TPU v7x, 32 devices: a whole 2x2x4 slice. The times are simulated.
32 devices in a mesh: dp: 16 (over z, x, core), mp: 2 (over y).
Axes of the slice: x: 2, y: 2, z: 4, core: 2. Of those that a mesh axis runs over, the one named last changes fastest.
Arguments:
- tokens: bfloat16 [25088, 768], P(('dp', 'mp')), may hold values from -6 to 6
- image_ids: int32 [25088], P('dp'), may hold values from -1 to 5, as said below
- rel_index: int32 [49, 49], replicated, may hold values from 0 to 168, as said below
- gain_one: bfloat16 [768], replicated, may hold values from 0.5 to 1.5
- shift_one: bfloat16 [768], replicated, may hold values from -3 to 3
- w_qkv: bfloat16 [768, 2304], P(None, 'mp'), may hold values from -0.21875 to 0.21875
- bias_query: bfloat16 [768], P('mp'), may hold values from -3 to 3
- bias_value: bfloat16 [768], P('mp'), may hold values from -3 to 3
- bias_table: bfloat16 [169, 24], P(None, 'mp'), may hold values from -4 to 4
- w_proj: bfloat16 [768, 768], P('mp'), may hold values from -0.5 to 0.5
- bias_proj: bfloat16 [768], replicated, may hold values from -2 to 2
- gain_two: bfloat16 [768], replicated, may hold values from 0.5 to 1.5
- shift_two: bfloat16 [768], replicated, may hold values from -3 to 3
- w_up: bfloat16 [768, 3072], P(None, 'mp'), may hold values from -0.21875 to 0.21875
- bias_up: bfloat16 [3072], P('mp'), may hold values from -3 to 3
- w_down: bfloat16 [3072, 768], P('mp'), may hold values from -0.109375 to 0.109375
- bias_down: bfloat16 [768], replicated, may hold values from -2 to 2
- cotangent: bfloat16 [25088, 768], P(('dp', 'mp')), may hold values from -6 to 6
Outputs:
- block_out: bfloat16 [25088, 768], P(('dp', 'mp'))
- grad_tokens: bfloat16 [25088, 768], P(('dp', 'mp'))
- grad_gain_one: float32 [768], replicated
- grad_shift_one: float32 [768], replicated
- grad_w_qkv: float32 [768, 2304], P(None, 'mp')
- grad_bias_query: float32 [768], P('mp')
- grad_bias_value: float32 [768], P('mp')
- grad_bias_table: float32 [169, 24], P(None, 'mp')
- grad_w_proj: float32 [768, 768], P('mp')
- grad_bias_proj: float32 [768], replicated
- grad_gain_two: float32 [768], replicated
- grad_shift_two: float32 [768], replicated
- grad_w_up: float32 [768, 3072], P(None, 'mp')
- grad_bias_up: float32 [3072], P('mp')
- grad_w_down: float32 [3072, 768], P('mp')
- grad_bias_down: float32 [768], replicated
Inputs may be any that keep to these rules, and one draw needn't show every extreme that they name: `image_ids`: in each window either all 49 slots hold 0 (one image), or five images of 9 slots hold 1 to 5 and 4 padding slots hold -1; the first window is of the second kind. rel_index[a, b] = (r_a - r_b + 6) * 13 + c_a - c_b + 6, where slot a sits at row r_a and column c_a of the window, each grid place taken by one slot.
All inputs are finite; a program needn't handle non-finite values.
Results may differ from a plain program's by a relative error of at most 0.018.
Values may be sent and summed in bfloat16 or wider, within the bound.
No kernel may reach another device: no remote copies, remote signals or barrier semaphores. Data moves between devices by JAX's collectives and lax.ppermute only.
A program may use at most 256 MiB of HBM per device.

v0:
```python
import jax
import jax.numpy as jnp
from jax import lax
from jax.sharding import PartitionSpec as P

HEAD_DIM = 32
SLOTS = 49


norm_eps = 1e-05
mask_fill = -1000000000.0
block_windows = 16


def layer_norm(values_in, gain_in, shift_in):
    row_mean = jnp.mean(values_in, axis=-1, keepdims=True)
    centred = values_in - row_mean
    spread = jnp.mean(centred * centred, axis=-1, keepdims=True)
    return centred * lax.rsqrt(spread + norm_eps) * gain_in + shift_in


def gelu_exact(values_in):
    return jax.nn.gelu(values_in, approximate=False)


def position_bias(rel_index, table_part):
    offsets = jnp.arange(table_part.shape[0], dtype=jnp.int32)
    onehot = (rel_index.reshape(-1, 1) == offsets[None, :]).astype(jnp.float32)
    flat = jnp.dot(
        onehot,
        table_part.astype(jnp.float32),
        precision=lax.Precision.HIGHEST,
        preferred_element_type=jnp.float32,
    )
    return (jnp.transpose(flat.reshape(SLOTS, SLOTS, -1), (2, 0, 1)), onehot)


def score_block(query_low, key_low, labels, pos_bias):
    raw_scores = jnp.einsum(
        "wqhd,wkhd->whqk", query_low, key_low, preferred_element_type=jnp.float32
    )
    scores = raw_scores * HEAD_DIM ** (-0.5) + pos_bias[None]
    same_image = labels[:, :, None] == labels[:, None, :]
    diagonal_ok = jnp.eye(SLOTS, dtype=bool)[None]
    allowed = same_image & ((labels[:, None, :] >= 0) | diagonal_ok)
    return jnp.where(allowed[:, None], scores, mask_fill)


def split_blocks(qkv_low, labels):
    row_count = qkv_low.shape[0]
    head_count = qkv_low.shape[1]
    windows = row_count // SLOTS
    shaped = qkv_low.reshape(
        windows // block_windows, block_windows, SLOTS, head_count, 3, HEAD_DIM
    )
    return (shaped, labels.reshape(windows // block_windows, block_windows, SLOTS))


def attention_forward(qkv_low, labels, pos_bias):
    shaped, label_blocks = split_blocks(qkv_low, labels)

    def one_block(packet):
        block, label_block = packet
        scores = score_block(block[..., 0, :], block[..., 1, :], label_block, pos_bias)
        row_max = jnp.max(scores, axis=-1, keepdims=True)
        exponent = jnp.exp(scores - row_max)
        denominator = jnp.sum(exponent, axis=-1, keepdims=True)
        weights_low = (exponent / denominator).astype(jnp.bfloat16)
        attended = jnp.einsum(
            "whqk,wkhd->wqhd", weights_low, block[..., 2, :], preferred_element_type=jnp.float32
        )
        return (attended.astype(jnp.bfloat16), (row_max + jnp.log(denominator))[..., 0])

    attended, log_total = lax.map(one_block, (shaped, label_blocks))
    return (attended.reshape(qkv_low.shape[0], -1), log_total)


def attention_backward(qkv_low, labels, pos_bias, grad_low, log_total):
    shaped, label_blocks = split_blocks(qkv_low, labels)
    grad_blocks = grad_low.reshape(
        shaped.shape[0], shaped.shape[1], SLOTS, shaped.shape[3], HEAD_DIM
    )

    def one_block(bias_sum, packet):
        block, label_block, grad_block, total_block = packet
        query_low = block[..., 0, :]
        key_low = block[..., 1, :]
        value_low = block[..., 2, :]
        scores = score_block(query_low, key_low, label_block, pos_bias)
        probability = jnp.exp(scores - total_block[..., None])
        grad_value = jnp.einsum(
            "whqk,wqhd->wkhd",
            probability.astype(jnp.bfloat16),
            grad_block,
            preferred_element_type=jnp.float32,
        )
        grad_prob = jnp.einsum(
            "wqhd,wkhd->whqk", grad_block, value_low, preferred_element_type=jnp.float32
        )
        grad_scores = probability * (
            grad_prob - jnp.sum(probability * grad_prob, axis=-1, keepdims=True)
        )
        grad_scores_low = grad_scores.astype(jnp.bfloat16)
        grad_query = jnp.einsum(
            "whqk,wkhd->wqhd", grad_scores_low, key_low, preferred_element_type=jnp.float32
        ) * HEAD_DIM ** (-0.5)
        grad_key = jnp.einsum(
            "whqk,wqhd->wkhd", grad_scores_low, query_low, preferred_element_type=jnp.float32
        ) * HEAD_DIM ** (-0.5)
        bias_sum = bias_sum + jnp.sum(grad_scores_low.astype(jnp.float32), axis=0)
        return (bias_sum, jnp.stack([grad_query, grad_key, grad_value], axis=3))

    start_sum = jnp.zeros(pos_bias.shape, jnp.float32)
    bias_sum, grads = lax.scan(one_block, start_sum, (shaped, label_blocks, grad_blocks, log_total))
    return (grads.reshape(qkv_low.shape[0], -1), bias_sum)


def on_device(
    tokens,
    image_ids,
    rel_index,
    gain_one,
    shift_one,
    w_qkv,
    bias_query,
    bias_value,
    bias_table,
    w_proj,
    bias_proj,
    gain_two,
    shift_two,
    w_up,
    bias_up,
    w_down,
    bias_down,
    cotangent,
):
    residual_in = tokens.astype(jnp.float32)
    gain_first = gain_one.astype(jnp.float32)
    shift_first = shift_one.astype(jnp.float32)
    gain_second = gain_two.astype(jnp.float32)
    shift_second = shift_two.astype(jnp.float32)
    low_one = layer_norm(residual_in, gain_first, shift_first).astype(jnp.bfloat16)
    weight_set = (w_qkv, bias_query, bias_value, bias_table, w_proj, w_up, bias_up, w_down)
    rows_one = lax.all_gather(low_one, "mp", axis=0, tiled=True)
    qkv_use, query_use, value_use, table_use, proj_use, up_use, up_bias_use, down_use = weight_set
    head_count = qkv_use.shape[1] // (3 * HEAD_DIM)
    qkv_raw = jnp.dot(rows_one, qkv_use, preferred_element_type=jnp.float32).reshape(
        -1, head_count, 3, HEAD_DIM
    )
    zero_block = jnp.zeros((head_count, HEAD_DIM), jnp.float32)
    qkv_bias = jnp.stack(
        [
            query_use.astype(jnp.float32).reshape(head_count, HEAD_DIM),
            zero_block,
            value_use.astype(jnp.float32).reshape(head_count, HEAD_DIM),
        ],
        axis=1,
    )
    qkv_low = (qkv_raw + qkv_bias[None]).astype(jnp.bfloat16)
    pos_bias, onehot = position_bias(rel_index, table_use)
    attended, log_total = attention_forward(qkv_low, image_ids, pos_bias)
    attn_sum = lax.psum_scatter(
        jnp.dot(attended, proj_use, preferred_element_type=jnp.float32),
        "mp",
        scatter_dimension=0,
        tiled=True,
    )
    middle = residual_in + attn_sum + bias_proj.astype(jnp.float32)
    low_two = layer_norm(middle, gain_second, shift_second).astype(jnp.bfloat16)
    rows_two = lax.all_gather(low_two, "mp", axis=0, tiled=True)
    pre_act = jnp.dot(rows_two, up_use, preferred_element_type=jnp.float32) + up_bias_use.astype(
        jnp.float32
    )
    hidden_low = gelu_exact(pre_act).astype(jnp.bfloat16)
    mlp_sum = lax.psum_scatter(
        jnp.dot(hidden_low, down_use, preferred_element_type=jnp.float32).astype(jnp.bfloat16),
        "mp",
        scatter_dimension=0,
        tiled=True,
    ).astype(jnp.float32)
    block_out = (middle + mlp_sum + bias_down.astype(jnp.float32)).astype(jnp.bfloat16)
    grad_result = cotangent.astype(jnp.float32)
    grad_bias_down = jnp.sum(grad_result, axis=0)
    grad_rows = lax.all_gather(cotangent, "mp", axis=0, tiled=True)
    grad_down = jnp.einsum("nf,nd->fd", hidden_low, grad_rows, preferred_element_type=jnp.float32)
    grad_hidden = jnp.einsum("nd,fd->nf", grad_rows, down_use, preferred_element_type=jnp.float32)
    gelu_unused, gelu_back = jax.vjp(gelu_exact, pre_act)
    grad_pre_low = gelu_back(grad_hidden)[0].astype(jnp.bfloat16)
    grad_up_bias = jnp.sum(grad_pre_low.astype(jnp.float32), axis=0)
    grad_up = jnp.einsum("nd,nf->df", rows_two, grad_pre_low, preferred_element_type=jnp.float32)
    grad_two = lax.psum_scatter(
        jnp.einsum("nf,df->nd", grad_pre_low, up_use, preferred_element_type=jnp.float32),
        "mp",
        scatter_dimension=0,
        tiled=True,
    )
    norm_unused, second_back = jax.vjp(layer_norm, middle, gain_second, shift_second)
    grad_mid_norm, grad_gain_two, grad_shift_two = second_back(grad_two)
    grad_middle = grad_result + grad_mid_norm
    grad_branch_low = grad_middle.astype(jnp.bfloat16)
    grad_bias_proj = jnp.sum(grad_branch_low.astype(jnp.float32), axis=0)
    grad_branch_rows = lax.all_gather(grad_branch_low, "mp", axis=0, tiled=True)
    grad_proj = jnp.einsum(
        "nc,nd->cd", attended, grad_branch_rows, preferred_element_type=jnp.float32
    )
    grad_attended = jnp.einsum(
        "nd,cd->nc", grad_branch_rows, proj_use, preferred_element_type=jnp.float32
    ).astype(jnp.bfloat16)
    grad_qkv, grad_pos = attention_backward(qkv_low, image_ids, pos_bias, grad_attended, log_total)
    grad_qkv_low = grad_qkv.astype(jnp.bfloat16)
    grad_parts = grad_qkv_low.astype(jnp.float32).reshape(-1, head_count, 3, HEAD_DIM)
    grad_query_b = jnp.sum(grad_parts[:, :, 0, :], axis=0).reshape(-1)
    grad_value_b = jnp.sum(grad_parts[:, :, 2, :], axis=0).reshape(-1)
    grad_pos_flat = jnp.transpose(grad_pos, (1, 2, 0)).reshape(SLOTS * SLOTS, head_count)
    grad_table = jnp.einsum(
        "sr,sh->rh",
        onehot,
        grad_pos_flat,
        precision=lax.Precision.HIGHEST,
        preferred_element_type=jnp.float32,
    )
    grad_qkv_w = jnp.einsum("nd,nc->dc", rows_one, grad_qkv_low, preferred_element_type=jnp.float32)
    grad_one = lax.psum_scatter(
        jnp.einsum("nc,dc->nd", grad_qkv_low, qkv_use, preferred_element_type=jnp.float32).astype(
            jnp.bfloat16
        ),
        "mp",
        scatter_dimension=0,
        tiled=True,
    ).astype(jnp.float32)
    norm_unused_first, first_back = jax.vjp(layer_norm, residual_in, gain_first, shift_first)
    grad_in_norm, grad_gain_one, grad_shift_one = first_back(grad_one)
    grad_tokens = (grad_middle + grad_in_norm).astype(jnp.bfloat16)
    (
        grad_qkv_w,
        grad_query_b,
        grad_value_b,
        grad_table,
        grad_proj,
        grad_up,
        grad_up_bias,
        grad_down,
    ) = (
        lax.psum(grad_qkv_w.astype(jnp.bfloat16), "dp").astype(jnp.float32),
        lax.psum(grad_query_b.astype(jnp.bfloat16), "dp").astype(jnp.float32),
        lax.psum(grad_value_b.astype(jnp.bfloat16), "dp").astype(jnp.float32),
        lax.psum(grad_table.astype(jnp.bfloat16), "dp").astype(jnp.float32),
        lax.psum(grad_proj.astype(jnp.bfloat16), "dp").astype(jnp.float32),
        lax.psum(grad_up.astype(jnp.bfloat16), "dp").astype(jnp.float32),
        lax.psum(grad_up_bias.astype(jnp.bfloat16), "dp").astype(jnp.float32),
        lax.psum(grad_down.astype(jnp.bfloat16), "dp").astype(jnp.float32),
    )
    grad_gain_one, grad_shift_one, grad_bias_proj, grad_gain_two, grad_shift_two, grad_bias_down = (
        lax.psum(
            (
                grad_gain_one,
                grad_shift_one,
                grad_bias_proj,
                grad_gain_two,
                grad_shift_two,
                grad_bias_down,
            ),
            ("dp", "mp"),
        )
    )
    return (
        block_out,
        grad_tokens,
        grad_gain_one,
        grad_shift_one,
        grad_qkv_w,
        grad_query_b,
        grad_value_b,
        grad_table,
        grad_proj,
        grad_bias_proj,
        grad_gain_two,
        grad_shift_two,
        grad_up,
        grad_up_bias,
        grad_down,
        grad_bias_down,
    )


def solution(mesh):
    return jax.shard_map(
        on_device,
        mesh=mesh,
        in_specs=(
            P(("dp", "mp"), None),
            P("dp"),
            P(),
            P(),
            P(),
            P(None, "mp"),
            P("mp"),
            P("mp"),
            P(None, "mp"),
            P("mp", None),
            P(),
            P(),
            P(),
            P(None, "mp"),
            P("mp"),
            P("mp", None),
            P(),
            P(("dp", "mp"), None),
        ),
        out_specs=(
            P(("dp", "mp"), None),
            P(("dp", "mp"), None),
            P(),
            P(),
            P(None, "mp"),
            P("mp"),
            P("mp"),
            P(None, "mp"),
            P("mp", None),
            P(),
            P(),
            P(),
            P(None, "mp"),
            P("mp"),
            P("mp", None),
            P(),
        ),
        check_vma=False,
    )
```

profile of v0, /device:TPU:0, one launch (start us, length us, event | category | flops | bytes accessed | tf_op | source)
XLA Modules:
  0.0 806.4 jit_solution(13251077336776903398)
XLA Ops:
  10.5 1.8 fusion.31
  17.3 37.2 %all-gather.5.cloned.1.call-done = bf16[1568,768]{1,0:T(8,128)(2,1)} async-done(((bf16[784,768]{1,0:T(8,128)(2,1)}), bf16[1568,768]{1,0:T(8,128)(2,1)}) %all-gather.5.cloned.1.call-update) | async-done | bytes 2408464 | tf_op jit(solution)/shard_map/all_gather | solution.py:145
  54.5 8.7 %fusion.48 = f32[1568,1152]{0,1:T(8,128)} fusion(bf16[1568,768]{1,0:T(8,128)(2,1)} %all-gather.5.cloned.1.call-done, bf16[768,1152]{1,0:T(8,128)(2,1)} %param.27), kind=kOutput, calls=%fused_computation.124 | convolution fusion | flops 2774532096 | bytes 11403264 | tf_op jit(solution)/shard_map/dot_general | solution.py:148
  63.2 29.2 %reshape.205 = f32[2,16,49,12,3,32]{2,1,0,5,4,3:T(8,128)} reshape(f32[1568,1152]{0,1:T(8,128)} %fusion.48) | data formatting | bytes 14450688 | tf_op jit(solution)/shard_map/reshape | solution.py:148
  92.4 10.1 %add_convert_fusion = bf16[2,16,49,12,3,32]{2,1,0,5,4,3:T(8,128)(2,1)} fusion(f32[2,16,49,12,3,32]{2,1,0,5,4,3:T(8,128)} %reshape.205, f32[12,3,32]{2,1,0:T(4,128)S(1)} %copy.74), kind=kLoop, calls=%fused_computation.45 | loop fusion | flops 3612672 | bytes 10842624 | tf_op jit(solution)/shard_map/convert_element_type | solution.py:160
  102.5 11.0 %copy.76 = bf16[2,16,49,12,3,32]{2,5,3,1,4,0:T(8,128)(2,1)} copy(bf16[2,16,49,12,3,32]{2,1,0,5,4,3:T(8,128)(2,1)} %add_convert_fusion) | data formatting | bytes 7225344 | tf_op jit(solution)/shard_map/while | solution.py:74
  113.4 26.7 %while.25 = (s32[]{:T(128)}, bf16[2,16,49,12,32]{2,1,0,4,3:T(8,128)(2,1)}, f32[2,16,12,49]{3,2,1,0:T(8,128)S(1)}, bf16[2,16,49,12,3,32]{2,5,3,1,4,0:T(8,128)(2,1...) while((s32[]{:T(128)}, bf16[2,16,49,12,32]{2,1,0,4,3:T(8,128)(2,1)}, ...), condition=%wide.region_5.6_spmd, body=%wide.region_2.5_spmd.sunk | while | flops 66331936 | bytes 32799632 | solution.py:74
  114.9 3.2 dynamic-slice_bitcast_fusion.10
  118.1 1.8 fusion.88
  119.9 2.1 fusion.89
  122.0 2.1 fusion.90
  128.0 3.2 dynamic-slice_bitcast_fusion.10
  131.2 1.8 fusion.88
  133.0 2.1 fusion.89
  135.2 2.1 fusion.90
  140.2 6.8 reshape.208
  147.0 4.9 fusion.49
  152.6 60.5 %reduce-scatter.5.cloned.1.call-done = f32[784,768]{1,0:T(8,128)} async-done(((f32[1568,768]{1,0:T(8,128)}), f32[784,768]{1,0:T(8,128)}) %reduce-scatter.5.cloned.1.call-update) | async-done | bytes 2408464 | tf_op jit(solution)/shard_map/reduce_scatter | solution.py:163
  213.2 2.4 fusion.45
  219.1 36.1 %all-gather.7.cloned.1.call-done = bf16[1568,768]{1,0:T(8,128)(2,1)} async-done(((bf16[784,768]{1,0:T(8,128)(2,1)}), bf16[1568,768]{1,0:T(8,128)(2,1)}) %all-gather.7.cloned.1.call-update) | async-done | bytes 2408464 | tf_op jit(solution)/shard_map/all_gather | solution.py:171
  255.3 27.2 %multiply_convert_fusion.1 = (bf16[1568,1536]{1,0:T(8,128)(2,1)}, f32[1568,1536]{1,0:T(8,128)}, f32[1568,1536]{1,0:T(8,128)}) fusion(f32[1536]{0:T(1024)S(1)} %convert_element_type.169, bf16[1568,768]{1,0:T(8,128)(2,1)} %all-gather.7.cloned.1.call-done, bf16[768,1536]{1,0:T(8,128)(2,1)S(1)} %copy-done), kind=kOutput, calls=%fused_computation.49 | convolution fusion | flops 3858333696 | bytes 28858368 | tf_op jit(solution)/shard_map/dot_general | solution.py:172
  282.4 11.0 %all-gather.9.cloned.1.call-done = bf16[1568,768]{1,0:T(8,128)(2,1)} async-done(((bf16[784,768]{1,0:T(8,128)(2,1)}), bf16[1568,768]{1,0:T(8,128)(2,1)}) %all-gather.9.cloned.1.call-update) | async-done | bytes 2408464 | tf_op jit(solution)/shard_map/all_gather | solution.py:185
  293.4 13.6 %fusion.47 = (bf16[1536]{0:T(1024)(128)(2,1)}, bf16[1568,1536]{1,0:T(8,128)(2,1)S(1)}) fusion(f32[1568,1536]{1,0:T(8,128)} %get-tuple-element.235, f32[1568,1536]{1,0:T(8,128)} %get-tuple-element.245, bf16[1568,768]{1,0:T(8,128)(2,1)} %all-gather.9.cloned.1.call-done, bf16[1536,768]{1,0:T(8,128)(2,1)} %param.37), kind=kOutput, calls=%fused_computation.123 | convolution fusion | flops 3735501312 | bytes 28855296 | tf_op jit(solution)/shard_map/nd,fd->nf/dot_general | solution.py:187
  307.0 2.2 copy-done.53
  309.2 5.5 fusion.50
  316.4 7.5 convolution_convert_fusion.4
  324.2 51.7 %reduce-scatter.9.cloned.1.call-done = f32[784,768]{1,0:T(8,128)} async-done(((f32[1568,768]{1,0:T(8,128)}), f32[784,768]{1,0:T(8,128)}) %reduce-scatter.9.cloned.1.call-update) | async-done | bytes 2408464 | tf_op jit(solution)/shard_map/reduce_scatter | solution.py:192
  376.0 3.9 multiply_reduce_fusion.1
  379.9 34.0 %reduce-scatter.7.cloned.1.call-done = bf16[784,768]{1,0:T(8,128)(2,1)} async-done(((bf16[1568,768]{1,0:T(8,128)(2,1)}), bf16[784,768]{1,0:T(8,128)(2,1)}) %reduce-scatter.7.cloned.1.call-update) | async-done | bytes 1204240 | tf_op jit(solution)/shard_map/reduce_scatter | solution.py:176
  413.9 4.8 fusion.43
  420.2 2.1 convert_reduce_fusion.4
  422.4 9.2 %convolution_convert_fusion.2 = bf16[1536,768]{1,0:T(8,128)(2,1)} fusion(bf16[1568,1536]{1,0:T(8,128)(2,1)} %get-tuple-element.234, bf16[1568,768]{1,0:T(8,128)(2,1)} %all-gather.9.cloned.1.call-done), kind=kOutput, calls=%fused_computation.78 | convolution fusion | flops 3700555776 | bytes 9584640 | tf_op jit(solution)/shard_map/nf,nd->fd/dot_general | solution.py:186
  431.6 8.3 %convolution_convert_fusion.3 = bf16[768,1536]{1,0:T(8,128)(2,1)} fusion(bf16[1568,768]{1,0:T(8,128)(2,1)S(1)} %copy-done.49, bf16[1568,1536]{1,0:T(8,128)(2,1)} %copy-done.53), kind=kOutput, calls=%fused_computation.79 | convolution fusion | flops 3700555776 | bytes 9584640 | tf_op jit(solution)/shard_map/nd,nf->df/dot_general | solution.py:191
  439.9 19.2 %all-gather.11.cloned.1.call-done = bf16[1568,768]{1,0:T(8,128)(2,1)} async-done(((bf16[784,768]{1,0:T(8,128)(2,1)}), bf16[1568,768]{1,0:T(8,128)(2,1)}) %all-gather.11.cloned.1.call-update) | async-done | bytes 2408464 | tf_op jit(solution)/shard_map/all_gather | solution.py:203
  459.1 4.1 convolution_convert_fusion.5
  463.2 1.8 copy.78
  465.0 10.2 %reshape.209 = bf16[2,16,49,12,32]{2,1,0,4,3:T(8,128)(2,1)} reshape(bf16[1568,384]{0,1:T(8,128)(2,1)S(1)} %copy.78) | data formatting | bytes 2408448 | tf_op jit(solution)/shard_map/reshape | solution.py:80
  475.2 42.7 %while.26 = (s32[]{:T(128)}, f32[12,49,49]{1,2,0:T(8,128)S(1)}, bf16[2,16,49,12,3,32]{2,5,3,1,4,0:T(8,128)(2,1)}, s32[2,16,49]{2,1,0:T(8,128)}, bf16[2,16,49,12,...) while((s32[]{:T(128)}, f32[12,49,49]{1,2,0:T(8,128)S(1)}, ...), condition=%wide.region_16.17_spmd.clone, body=%wide.region_13.16_spmd.clone.sunk | while | flops 159810416 | bytes 91269600 | solution.py:114
  476.7 1.7 constant_dynamic-slice_fusion.2
  478.4 3.2 dynamic-slice_bitcast_fusion.11
  483.2 2.6 multiply_reduce_fusion.5
  493.1 3.6 copy-done.8
  499.5 3.2 dynamic-slice_bitcast_fusion.11
  504.3 2.6 multiply_reduce_fusion.5
  514.1 3.6 copy-done.8
  517.9 18.3 %copy.81 = bf16[2,16,49,12,3,32]{2,1,0,5,4,3:T(8,128)(2,1)} copy(bf16[2,16,49,12,3,32]{2,5,3,1,4,0:T(8,128)(2,1)} %get-tuple-element.94) | data formatting | bytes 7225344 | tf_op jit(solution)/shard_map/convert_element_type | solution.py:211
  536.2 16.4 %convert_element_type.180 = bf16[1568,1152]{0,1:T(8,128)(2,1)} reshape(bf16[2,16,49,12,3,32]{2,1,0,5,4,3:T(8,128)(2,1)} %copy.81) | data formatting | bytes 7225344 | tf_op jit(solution)/shard_map/convert_element_type | solution.py:211
  552.5 3.9 convolution_convert_fusion.6
  556.4 5.0 convolution_convert_fusion
  562.9 6.9 convolution_convert_fusion.1
  569.8 21.5 %copy.82 = f32[2,16,49,12,3,32]{2,1,0,5,4,3:T(8,128)} copy(bf16[2,16,49,12,3,32]{2,5,3,1,4,0:T(8,128)(2,1)} %get-tuple-element.94) | data formatting | bytes 10838016 | tf_op jit(solution)/shard_map/convert_element_type | solution.py:212
  591.6 18.7 %reshape.213 = f32[1568,12,3,32]{0,3,2,1:T(8,128)} reshape(f32[2,16,49,12,3,32]{2,1,0,5,4,3:T(8,128)} %copy.82) | data formatting | bytes 14450688 | tf_op jit(solution)/shard_map/convert_element_type | solution.py:212
  610.4 2.9 slice_reduce_fusion
  614.4 62.1 %all-reduce.1 = (bf16[384]{0:T(512)(128)(2,1)S(1)}, bf16[384]{0:T(512)(128)(2,1)S(1)}, bf16[169,12]{0,1:T(8,128)(2,1)S(1)}, bf16[1536]{0:T(1024)(128)(2,1)S(1)}) all-reduce(bf16[384]{0:T(512)(128)(2,1)S(1)} %convert_element_type.189, bf16[384]{0:T(512)(128)(2,1)S(1)} %convert_element_type.192, ...), channel_id=1, replica_groups=mesh['dp'=16,'mp'=2] {'dp'}, use_global_device_ids=true, to_apply=%region_26.27 | all-reduce | flops 4332 | bytes 17328 | tf_op jit(solution)/shard_map/psum | solution.py:246
  678.9 34.6 %all-reduce.5.cloned.1.call-done = (bf16[768,1152]{1,0:T(8,128)(2,1)}, bf16[384,768]{1,0:T(8,128)(2,1)}, bf16[768,1536]{1,0:T(8,128)(2,1)}, bf16[1536,768]{1,0:T(8,128)(2,1)}) async-done(((bf16[768,1152]{1,0:T(8,128)(2,1)}, bf16[384,768]{1,0:T(8,128)(2,1)}, bf16[768,1536]{1,0:T(8,128)(2,1)}, bf16[1536,768]{1,0:T(8,128)(2,1)}), (bf16[768,1152]{1,0:T(8,128)(2,1)}, bf16[384,768]{1,0:T(8,128)(2,1)}, ...) | async-done | bytes 7077904 | tf_op jit(solution)/shard_map/psum | solution.py:245
  713.4 2.3 convert_element_type.197
  715.7 2.0 convert_element_type.185
  718.5 2.8 convert_element_type.200
  721.4 2.5 convert_element_type.203
  723.9 27.2 %reduce-scatter.11.cloned.1.call-done = bf16[784,768]{1,0:T(8,128)(2,1)} async-done(((bf16[1568,768]{1,0:T(8,128)(2,1)}), bf16[784,768]{1,0:T(8,128)(2,1)}) %reduce-scatter.11.cloned.1.call-update) | async-done | bytes 1204240 | tf_op jit(solution)/shard_map/reduce_scatter | solution.py:224
  751.1 2.3 convert_reduce_fusion.1
  753.5 2.7 fusion.34
  756.3 3.4 convert_reduce_fusion.3
  759.7 40.0 %all-reduce = (f32[768]{0:T(1024)}, f32[768]{0:T(1024)}, f32[768]{0:T(1024)}, f32[768]{0:T(1024)}, f32[768]{0:T(1024)}, /*index=5*/f32[768]{0:T(1024)}) all-reduce(f32[768]{0:T(1024)S(1)} %get-tuple-element.177, f32[768]{0:T(1024)S(1)} %get-tuple-element.180, f32[768]{0:T(1024)S(1)} %copy-done.36, ...), channel_id=1, replica_groups=mesh['dp'=16,'mp'=2] {'dp','mp'}, use_global_device_ids=true, to_apply=%region_21.22 | all-reduce | flops 4608 | bytes 36864 | tf_op jit(solution)/shard_map/psum | solution.py:255
  (218 shorter events, 51.0 us)
Async XLA Ops:
  7.2 248.1 %copy-start = (bf16[768,1536]{1,0:T(8,128)(2,1)S(1)}, bf16[768,1536]{1,0:T(8,128)(2,1)}, u32[]{:S(2)}) copy-start(bf16[768,1536]{1,0:T(8,128)(2,1)} %param.35) | copy-start | bytes 7077892
  7.2 47.3 %all-gather.5.cloned.1.call-start = ((), (), s32[]{:S(2)}) async-start(), calls=%async_computation.4 | async-start | bytes 3612672 | tf_op jit(solution)/shard_map/all_gather | solution.py:145
  7.2 6.2 copy-start.3
  8.1 4.8 copy-start.25
  8.8 6.2 copy-start.46
  8.8 6.3 copy-start.47
  10.4 5.0 copy-start.33
  10.4 5.1 copy-start.39
  10.4 5.9 copy-start.52
  10.4 2.4 copy-start.23
  15.0 198.2 %reduce-scatter.5.cloned.1.call-start = ((), (), s32[]{:S(2)}) async-start(), calls=%async_computation.5 | async-start | bytes 7225344 | tf_op jit(solution)/shard_map/reduce_scatter | solution.py:163
  122.0 2.2 copy-start.15
  125.3 1.7 copy-start.16
  135.2 2.2 copy-start.15
  138.5 1.7 copy-start.16
  140.2 11.8 %copy-start.6 = (f32[12,49,49]{1,2,0:T(8,128)}, f32[12,49,49]{1,2,0:T(8,128)S(1)}, u32[]{:S(2)}) copy-start(f32[12,49,49]{1,2,0:T(8,128)S(1)} %get-tuple-element.422) | copy-start | bytes 345748
  140.2 11.8 %copy-start.20 = (f32[2,16,12,49]{3,2,1,0:T(8,128)}, f32[2,16,12,49]{3,2,1,0:T(8,128)S(1)}, u32[]{:S(2)}) copy-start(f32[2,16,12,49]{3,2,1,0:T(8,128)S(1)} %get-tuple-element.381) | copy-start | bytes 225796
  140.2 6.8 copy-start.22
  152.0 103.3 %all-gather.7.cloned.1.call-start = ((), (), s32[]{:S(2)}) async-start(), calls=%async_computation.6 | async-start | bytes 3612672 | tf_op jit(solution)/shard_map/all_gather | solution.py:171
  217.0 2.1 copy-start.40
  218.5 74.9 %all-gather.9.cloned.1.call-start = ((), (), s32[]{:S(2)}) async-start(), calls=%async_computation.8 | async-start | bytes 3612672 | tf_op jit(solution)/shard_map/all_gather | solution.py:185
  219.1 156.9 %reduce-scatter.9.cloned.1.call-start = ((), (), s32[]{:S(2)}) async-start(), calls=%async_computation.9 | async-start | bytes 7225344 | tf_op jit(solution)/shard_map/reduce_scatter | solution.py:192
  307.0 2.2 copy-start.53
  314.7 1.7 copy-start.50
  314.7 99.2 %reduce-scatter.7.cloned.1.call-start = ((), (), s32[]{:S(2)}) async-start(), calls=%async_computation.7 | async-start | bytes 3612672 | tf_op jit(solution)/shard_map/reduce_scatter | solution.py:176
  316.4 7.8 copy-start.45
  323.9 135.1 %all-gather.11.cloned.1.call-start = ((), (), s32[]{:S(2)}) async-start(), calls=%async_computation.10 | async-start | bytes 3612672 | tf_op jit(solution)/shard_map/all_gather | solution.py:203
  379.9 40.3 %copy-start.12 = (bf16[784,768]{1,0:T(8,128)(2,1)S(1)}, bf16[784,768]{1,0:T(8,128)(2,1)}, u32[]{:S(2)}) copy-start(bf16[784,768]{1,0:T(8,128)(2,1)} %param.39) | copy-start | bytes 3612676
  418.8 3.5 copy-start.29
  422.3 291.1 %all-reduce.5.cloned.1.call-start = ((), (), s32[]{:S(2)}) async-start(), calls=%async_computation.12 | async-start | bytes 14155776 | tf_op jit(solution)/shard_map/psum | solution.py:245
  422.4 9.2 %copy-start.49 = (bf16[1568,768]{1,0:T(8,128)(2,1)S(1)}, bf16[1568,768]{1,0:T(8,128)(2,1)}, u32[]{:S(2)}) copy-start(bf16[1568,768]{1,0:T(8,128)(2,1)} %all-gather.7.cloned.1.call-done) | copy-start | bytes 7225348
  465.0 10.2 %copy-start.7 = (f32[12,49,49]{1,2,0:T(8,128)S(1)}, f32[12,49,49]{1,2,0:T(8,128)}, u32[]{:S(2)}) copy-start(f32[12,49,49]{1,2,0:T(8,128)} %copy-done.6) | copy-start | bytes 345748
  465.0 10.2 %copy-start.21 = (f32[2,16,12,49]{3,2,1,0:T(8,128)S(1)}, f32[2,16,12,49]{3,2,1,0:T(8,128)}, u32[]{:S(2)}) copy-start(f32[2,16,12,49]{3,2,1,0:T(8,128)} %copy-done.20) | copy-start | bytes 225796
  487.1 4.2 slice-start
  487.2 4.2 slice-start.1
  488.8 2.6 slice-start.2
  493.0 3.7 copy-start.8
  508.2 4.2 slice-start
  508.2 4.2 slice-start.1
  509.8 2.6 slice-start.2
  514.1 3.7 copy-start.8
  536.2 16.4 %copy-start.13 = (bf16[1568,384]{0,1:T(8,128)(2,1)S(1)}, bf16[1568,384]{0,1:T(8,128)(2,1)}, u32[]{:S(2)}) copy-start(bf16[1568,384]{0,1:T(8,128)(2,1)} %reshape.208) | copy-start | bytes 3612676
  552.5 3.9 copy-start.14
  552.5 3.9 copy-start.48
  561.4 1.5 copy-start.51
  561.4 189.7 %reduce-scatter.11.cloned.1.call-start = ((), (), s32[]{:S(2)}) async-start(), calls=%async_computation.11 | async-start | bytes 3612672 | tf_op jit(solution)/shard_map/reduce_scatter | solution.py:224
  610.4 3.1 copy-start.38
  610.4 4.0 copy-start.41
  713.4 2.3 copy-start.19
  715.7 2.8 copy-start.18
  718.5 2.8 copy-start.17
  721.3 29.8 %copy-start.4 = (bf16[784,768]{1,0:T(8,128)(2,1)S(1)}, bf16[784,768]{1,0:T(8,128)(2,1)}, u32[]{:S(2)}) copy-start(bf16[784,768]{1,0:T(8,128)(2,1)} %param.22) | copy-start | bytes 3612676
  721.3 29.8 %copy-start.24 = (f32[784]{0:T(1024)S(1)}, f32[784]{0:T(1024)}, u32[]{:S(2)}) copy-start(f32[784]{0:T(1024)} %copy-done.23) | copy-start | bytes 9412
  721.3 29.8 %copy-start.26 = (f32[768]{0:T(1024)S(1)}, f32[768]{0:T(1024)}, u32[]{:S(2)}) copy-start(f32[768]{0:T(1024)} %copy-done.25) | copy-start | bytes 9220
  721.3 32.1 %copy-start.32 = (f32[784]{0:T(1024)S(1)}, f32[784]{0:T(1024)}, u32[]{:S(2)}) copy-start(f32[784]{0:T(1024)} %copy-done.31) | copy-start | bytes 9412
  721.4 32.1 %copy-start.28 = (f32[784]{0:T(1024)S(1)}, f32[784]{0:T(1024)}, u32[]{:S(2)}) copy-start(f32[784]{0:T(1024)} %copy-done.27) | copy-start | bytes 9412
  723.9 32.3 %copy-start.30 = (f32[784]{0:T(1024)S(1)}, f32[784]{0:T(1024)}, u32[]{:S(2)}) copy-start(f32[784]{0:T(1024)} %copy-done.29) | copy-start | bytes 9412
  751.1 5.1 copy-start.5
  751.1 5.1 copy-start.10
  751.1 5.1 copy-start.11
  756.2 43.5 %copy-start.1 = (bf16[768,1536]{1,0:T(8,128)(2,1)S(1)}, bf16[768,1536]{1,0:T(8,128)(2,1)}, u32[]{:S(2)}) copy-start(bf16[768,1536]{1,0:T(8,128)(2,1)} %param.35) | copy-start | bytes 7077892
  756.2 3.4 copy-start.34
  756.3 3.4 copy-start.35
  756.3 3.4 copy-start.36
  (8 other events, 6.9 us)
Sparse Core Ops, SparseCore 0:
  15.1 39.3 all-gather.4
  152.1 61.0 reduce-scatter.4
  218.6 36.6 all-gather.6
  256.8 36.6 all-gather.8
  314.9 61.0 reduce-scatter.8
  378.7 35.2 reduce-scatter.6
  422.4 36.6 all-gather.10
  561.5 151.8 all-reduce.4
  715.8 35.2 reduce-scatter.10
where the time goes:
time: 816 us; the launch traced here: 806 us
  waiting for transfers between devices  312 us (38%)
  local copies, waits for them, and re-layouts  175 us (21%)
  matrix products  131 us (16%)
  blocking collectives  102 us (12%)
  other arithmetic  69.7 us (9%)
  between operations  14.5 us (2%)
    psum x1, blocking collectives, on_device(): lax.psum(grad_query_b.astype(jnp.bfloat16), 'dp').astype(jnp.float32)  62.1 us
    reduce_scatter x1, waiting for transfers between devices, on_device(): lax.psum_scatter(jnp.dot(attended, proj_use, preferred_element_type=jnp.f...  60.5 us
    reduce_scatter x1, waiting for transfers between devices, on_device(): lax.psum_scatter(jnp.einsum('nf,df->nd', grad_pre_low, up_use, preferred_...  51.7 us
    convert_element_type x2, local copies, waits for them, and re-layouts, on_device(): grad_qkv_low.astype(jnp.float32).reshape(-1, head_count, 3, HEAD_DIM)  40.2 us
    psum x1, blocking collectives, on_device(): lax.psum((grad_gain_one, grad_shift_one, grad_bias_proj, grad_gain_two, g...  40 us
    all_gather x1, waiting for transfers between devices, on_device(): rows_one = lax.all_gather(low_one, 'mp', axis=0, tiled=True)  37.2 us
    all_gather x1, waiting for transfers between devices, on_device(): rows_two = lax.all_gather(low_two, 'mp', axis=0, tiled=True)  36.1 us
    convert_element_type x2, local copies, waits for them, and re-layouts, on_device(): grad_qkv_low = grad_qkv.astype(jnp.bfloat16)  34.6 us
  transfers between devices with their start and end apart: 9, of which 9 were waited for; matrix products, arithmetic and copies ran while one was open for 15% of the time, Pallas kernels for 0%

commit v1 on v0

v1 whole, which is shorter than its diff:
```python
import functools

import jax
import jax.numpy as jnp
from jax import lax
from jax.experimental import pallas as pl
from jax.experimental.pallas import tpu as pltpu
from jax.sharding import PartitionSpec as P

HEAD_DIM = 32
SLOTS = 49
PAD = 64
KEYS = 56
GROUP = 4
SPARE = 16
norm_eps = 1e-05
mask_fill = -1000000000.0
f32 = jnp.float32
bf16 = jnp.bfloat16
MIB = 1024 * 1024


def params(limit=56):
    return pltpu.CompilerParams(vmem_limit_bytes=limit * MIB)


def whole(shape):
    return pl.BlockSpec(shape, lambda *_: (0,) * len(shape))


def dot(left, right, dims=((1,), (0,))):
    return lax.dot_general(left, right, (dims, ((), ())), preferred_element_type=f32)


NT = ((1,), (1,))
TN = ((0,), (0,))


def norm_parts(values):
    mean = jnp.mean(values, axis=-1, keepdims=True)
    centred = values - mean
    spread = jnp.mean(centred * centred, axis=-1, keepdims=True)
    return centred, lax.rsqrt(spread + norm_eps)


def norm_back(values, gain, grad):
    centred, inverse = norm_parts(values)
    unit = centred * inverse
    scaled = grad * gain
    first = jnp.mean(scaled, axis=-1, keepdims=True)
    second = jnp.mean(scaled * unit, axis=-1, keepdims=True)
    return inverse * (scaled - first - unit * second), grad * unit


def col_sum(values):
    return jnp.sum(values, axis=0, keepdims=True)


def row_blocks(rows):
    size = 256 if rows % 16 == 0 else rows
    starts = list(range(0, rows, size))
    if len(starts) > 1 and rows - starts[-1] < 128:
        starts.pop()
    return [(s, (starts[i + 1] if i + 1 < len(starts) else rows) - s) for i, s in enumerate(starts)]


def diagonal(rows_of_heads):
    lane = lax.broadcasted_iota(jnp.int32, (PAD, 128), 1)
    out = rows_of_heads[3 * PAD :]
    for head in (2, 1, 0):
        out = jnp.where(lane < (head + 1) * HEAD_DIM, rows_of_heads[head * PAD : (head + 1) * PAD], out)
    return out


def spread(rows, block_mask):
    return jnp.concatenate([rows] * GROUP, axis=0) * block_mask


def block_mask_of():
    row = lax.broadcasted_iota(jnp.int32, (GROUP * PAD, 128), 0) // PAD
    lane = lax.broadcasted_iota(jnp.int32, (GROUP * PAD, 128), 1) // HEAD_DIM
    return (row == lane).astype(f32).astype(bf16)


def window_rows_mask(rows, cols):
    return lax.rem(lax.broadcasted_iota(jnp.int32, (rows, cols), 0), PAD) < SLOTS


def batch_of(windows):
    return 8 if windows % 8 == 0 else windows


def step_rows(ref, step, batch):
    if batch % 8:
        return ref
    return ref.at[pl.ds(pl.multiple_of(step * batch * SLOTS, 8), batch * SLOTS + SPARE)]


def pad_windows(src, dst, step, batch):
    view = step_rows(src, step, batch)
    for j in range(batch):
        dst[j * PAD : (j + 1) * PAD, :] = view[j * SLOTS : j * SLOTS + PAD, :].astype(bf16)


def fwd_kernel(groups, tokens, gain, shift, w, bias, pos, mask, qkv, probs, att, wp, padded, normed, att_s):
    step = pl.program_id(0)
    rows = tokens.shape[0]

    @pl.when(step == 0)
    def _():
        centred, inverse = norm_parts(tokens[...].astype(f32))
        value = (centred * inverse * gain[...] + shift[...]).astype(bf16)
        normed[0:rows, :] = value.astype(f32)
        normed[rows:, :] = jnp.zeros_like(normed[rows:, :])
        order = group_order()
        for g in range(groups):
            wp[:, g * 384 : (g + 1) * 384] = dot(w[:, g * 384 : (g + 1) * 384], order).astype(bf16)

    batch = mask.shape[0]
    pad_windows(normed, padded, step, batch)
    att_view = step_rows(att_s, step, batch)
    block_mask = block_mask_of()
    keep = window_rows_mask(batch * PAD, 384)
    left = padded[...]
    for g in range(groups):
        cols = slice(g * 384, (g + 1) * 384)
        value = dot(left, wp[:, cols]) + bias[:, cols]
        qkv[:, cols] = jnp.where(keep, value, 0.0).astype(bf16)
    for j in range(batch):
        rows_at = slice(j * PAD, (j + 1) * PAD)
        allowed = mask[j] > 0.0
        allowed = jnp.concatenate([allowed, allowed], axis=1)
        for g in range(groups):
            at = g * 384
            query = qkv[rows_at, at : at + 128]
            key = qkv[rows_at, at + 128 : at + 256]
            value = qkv[rows_at, at + 256 : at + 384]
            raw = dot(key, spread(query, block_mask), NT)[:KEYS]
            scores = raw * HEAD_DIM ** (-0.5) + pos[:, g * 256 : (g + 1) * 256]
            scores = jnp.where(allowed, scores, mask_fill)
            top = jnp.max(scores, axis=0, keepdims=True)
            power = jnp.exp(scores - top)
            total = jnp.sum(power, axis=0, keepdims=True)
            prob = power * (1.0 / total)
            prob = jnp.concatenate([prob, jnp.zeros((PAD - KEYS, 256), f32)], axis=0).astype(bf16)
            probs[j, :, g * 256 : (g + 1) * 256] = prob
            out = diagonal(dot(prob, value, TN))
            att_view[j * SLOTS : j * SLOTS + KEYS, g * 128 : (g + 1) * 128] = out[:KEYS]

    @pl.when(step == pl.num_programs(0) - 1)
    def _():
        windows = pl.num_programs(0) * batch
        value = att_s[0:rows, :]
        real = lax.broadcasted_iota(jnp.int32, value.shape, 0) < windows * SLOTS
        att[...] = jnp.where(real, value, 0.0).astype(bf16)


def attention_forward(tokens, gain, shift, w, bias, pos, mask):
    rows, width = tokens.shape
    windows = mask.shape[0]
    cols = w.shape[1]
    groups = cols // 384
    heads = groups * GROUP
    batch = batch_of(windows)
    steps = windows // batch
    quad_rows = batch * PAD
    out_shape = (
        jax.ShapeDtypeStruct((windows * PAD, cols), bf16),
        jax.ShapeDtypeStruct((windows, PAD, heads * PAD), bf16),
        jax.ShapeDtypeStruct((rows, heads * HEAD_DIM), bf16),
        jax.ShapeDtypeStruct((width, cols), bf16),
        jax.ShapeDtypeStruct((windows * PAD, width), bf16),
    )
    return pl.pallas_call(
        functools.partial(fwd_kernel, groups),
        grid=(steps,),
        in_specs=[
            whole((rows, width)),
            whole((1, width)),
            whole((1, width)),
            whole((width, cols)),
            whole((1, cols)),
            whole((KEYS, heads * PAD)),
            pl.BlockSpec((batch, KEYS, 128), lambda i: (i, 0, 0)),
        ],
        out_specs=[
            pl.BlockSpec((quad_rows, cols), lambda i: (i, 0)),
            pl.BlockSpec((batch, PAD, heads * PAD), lambda i: (i, 0, 0)),
            whole((rows, heads * HEAD_DIM)),
            whole((width, cols)),
            pl.BlockSpec((quad_rows, width), lambda i: (i, 0)),
        ],
        out_shape=out_shape,
        scratch_shapes=[
            pltpu.VMEM((rows + SPARE, width), f32),
            pltpu.VMEM((rows + SPARE, heads * HEAD_DIM), f32),
        ],
        compiler_params=params(),
        cost_estimate=pl.CostEstimate(
            flops=2 * windows * PAD * width * cols + 16 * windows * groups * 256 * 256 * 64,
            bytes_accessed=windows * PAD * cols * 4 + width * cols * 4,
            transcendentals=0,
        ),
        name="attention_forward",
    )(tokens, gain, shift, w, bias, pos, mask)


def proj_kernel(parts, *refs):
    atts, ws = refs[:parts], refs[parts : 2 * parts]
    tokens, bias, gain, shift, middle, low = refs[2 * parts :]
    for start, size in row_blocks(tokens.shape[0]):
        at = slice(start, start + size)
        value = tokens[at, :].astype(f32) + bias[...]
        for a, w in zip(atts, ws):
            value = value + dot(a[at, :], w[...])
        middle[at, :] = value
        centred, inverse = norm_parts(value)
        low[at, :] = (centred * inverse * gain[...] + shift[...]).astype(bf16)


def project(atts, ws, tokens, bias, gain, shift):
    rows, width = tokens.shape
    return pl.pallas_call(
        functools.partial(proj_kernel, len(atts)),
        out_shape=(jax.ShapeDtypeStruct((rows, width), f32), jax.ShapeDtypeStruct((rows, width), bf16)),
        compiler_params=params(),
        cost_estimate=pl.CostEstimate(flops=2 * rows * width * width, bytes_accessed=rows * width * 10, transcendentals=0),
        name="project",
    )(*atts, *ws, tokens, bias, gain, shift)


def gelu_parts(x):
    z = jnp.abs(x) * 0.7071067811865476
    t = 1.0 / (1.0 + 0.3275911 * z)
    e = jnp.exp(-z * z)
    half = t * (0.127414796 + t * (-0.142248368 + t * (0.7107068705 + t * (-0.7265760135 + t * 0.5307027145)))) * e
    cdf = jnp.where(x >= 0.0, 1.0 - half, half)
    return cdf, e * 0.3989422804014327


def mlp_kernel(first, last, order, *refs):
    low, dy, up, bias, down = refs[:5]
    refs = refs[5:]
    if not first:
        out_in, two_in = refs[:2]
        refs = refs[2:]
    if last:
        middle, bias_down, gain = refs[:3]
        refs = refs[3:]
        hidden, gpre, gbias, block_out, grad_middle, branch, sums, acc_out, acc_two = refs
    else:
        hidden, gpre, gbias, acc_out, acc_two = refs
    step = pl.program_id(0)
    rows = low.shape[0]

    @pl.when(step == 0)
    def _():
        if first:
            acc_out[...] = jnp.zeros_like(acc_out)
            acc_two[...] = jnp.zeros_like(acc_two)
        else:
            acc_out[...] = out_in[...]
            acc_two[...] = two_in[...]

    total = jnp.zeros(gbias.shape[1:], f32)
    for start, size in row_blocks(rows):
        at = slice(start, start + size)
        pre = dot(low[at, :], up[...], NT) + bias[0]
        back = dot(dy[at, :], down[...], NT)
        cdf, pdf = gelu_parts(pre)
        hid = (pre * cdf).astype(bf16)
        gp = (back * (cdf + pre * pdf)).astype(bf16)
        hidden[at, :] = hid
        gpre[at, :] = gp
        total = total + col_sum(gp.astype(f32))
        acc_out[at, :] += dot(hid, down[...])
        acc_two[at, :] += dot(gp, up[...])
    gbias[0] = total

    if last:

        @pl.when(step == pl.num_programs(0) - 1)
        def _():
            s_gain = s_shift = s_branch = s_down = jnp.zeros((1, low.shape[1]), f32)
            for start, size in row_blocks(rows):
                at = slice(start, start + size)
                mid = middle[at, :]
                block_out[at, :] = (mid + acc_out[at, :] + bias_down[...]).astype(bf16)
                two = acc_two[at, :]
                up_grad = dy[at, :].astype(f32)
                grad, for_gain = norm_back(mid, gain[...], two)
                grad = grad + up_grad
                grad_middle[at, :] = grad
                low_grad = grad.astype(bf16)
                branch[at, :] = low_grad
                s_gain += col_sum(for_gain)
                s_shift += col_sum(two)
                s_branch += col_sum(low_grad.astype(f32))
                s_down += col_sum(up_grad)
            sums[...] = jnp.concatenate([s_gain, s_shift, s_branch, s_down], axis=0)


def mlp(order, low, dy, up, bias, down, carried=None, finish=None):
    rows, width = low.shape
    units = up.shape[0]
    piece = bias.shape[2]
    steps = units // piece
    first, last = carried is None, finish is not None
    ins = [low, dy, up, bias, down]
    specs = [
        whole((rows, width)),
        whole((rows, width)),
        pl.BlockSpec((piece, width), lambda i, o: (i, 0)),
        pl.BlockSpec((1, 1, piece), lambda i, o: (o[i], 0, 0)),
        pl.BlockSpec((piece, width), lambda i, o: (i, 0)),
    ]
    outs = [
        jax.ShapeDtypeStruct((rows, units), bf16),
        jax.ShapeDtypeStruct((rows, units), bf16),
        jax.ShapeDtypeStruct(bias.shape, f32),
    ]
    out_specs = [
        pl.BlockSpec((rows, piece), lambda i, o: (0, i)),
        pl.BlockSpec((rows, piece), lambda i, o: (0, i)),
        pl.BlockSpec((1, 1, piece), lambda i, o: (o[i], 0, 0)),
    ]
    scratch = []
    if not first:
        ins += list(carried)
        specs += [whole((rows, width))] * 2
    if last:
        ins += list(finish)
        specs += [whole((rows, width)), whole((1, width)), whole((1, width))]
        outs += [
            jax.ShapeDtypeStruct((rows, width), bf16),
            jax.ShapeDtypeStruct((rows, width), f32),
            jax.ShapeDtypeStruct((rows, width), bf16),
            jax.ShapeDtypeStruct((4, width), f32),
        ]
        out_specs += [whole((rows, width))] * 3 + [whole((4, width))]
        scratch = [pltpu.VMEM((rows, width), f32)] * 2
    else:
        outs += [jax.ShapeDtypeStruct((rows, width), f32)] * 2
        out_specs += [whole((rows, width))] * 2
    return pl.pallas_call(
        functools.partial(mlp_kernel, first, last),
        grid_spec=pltpu.PrefetchScalarGridSpec(
            num_scalar_prefetch=1, grid=(steps,), in_specs=specs, out_specs=out_specs, scratch_shapes=scratch
        ),
        out_shape=tuple(outs),
        compiler_params=params(),
        cost_estimate=pl.CostEstimate(flops=8 * rows * width * units, bytes_accessed=rows * units * 4, transcendentals=0),
        name="mlp",
    )(order, *ins)


def bwd_kernel(groups, branch, wproj, qkv, probs, gqkv, bias_sum, col_sums, wide, padded):
    step = pl.program_id(0)
    rows = branch.shape[0]

    @pl.when(step == 0)
    def _():
        wide[0:rows, :] = branch[...].astype(f32)
        wide[rows:, :] = jnp.zeros_like(wide[rows:, :])
        bias_sum[...] = jnp.zeros_like(bias_sum)
        col_sums[...] = jnp.zeros_like(col_sums)

    batch = probs.shape[0]
    pad_windows(wide, padded, step, batch)
    block_mask = block_mask_of()
    scale = HEAD_DIM ** (-0.5)
    grads = dot(padded[...], wproj[...], NT)
    grads = jnp.where(window_rows_mask(batch * PAD, grads.shape[1]), grads, 0.0).astype(bf16)
    for g in range(groups):
        at = g * 384
        bias_total = jnp.zeros((KEYS, 256), f32)
        col_total = [jnp.zeros((1, 128), f32)] * 2
        for j in range(batch):
            rows_at = slice(j * PAD, (j + 1) * PAD)
            query = qkv[rows_at, at : at + 128]
            key = qkv[rows_at, at + 128 : at + 256]
            value = qkv[rows_at, at + 256 : at + 384]
            prob_low = probs[j, :, g * 256 : (g + 1) * 256]
            grad = spread(grads[rows_at, g * 128 : (g + 1) * 128], block_mask)
            prob = prob_low.astype(f32)[:KEYS]
            prob_grad = dot(value, grad, NT)[:KEYS]
            both = prob * prob_grad
            score_grad = both - prob * jnp.sum(both, axis=0, keepdims=True)
            score_grad = jnp.concatenate([score_grad, jnp.zeros((PAD - KEYS, 256), f32)], axis=0).astype(bf16)
            bias_total = bias_total + score_grad.astype(f32)[:KEYS]
            grad_value = dot(prob_low, grad).astype(bf16)
            grad_key = (dot(score_grad, spread(query, block_mask)) * scale).astype(bf16)
            grad_query = (diagonal(dot(score_grad, key, TN)) * scale).astype(bf16)
            gqkv[rows_at, at : at + 128] = grad_query
            gqkv[rows_at, at + 128 : at + 256] = grad_key
            gqkv[rows_at, at + 256 : at + 384] = grad_value
            col_total[0] = col_total[0] + col_sum(grad_query.astype(f32))
            col_total[1] = col_total[1] + col_sum(grad_value.astype(f32))
        bias_sum[:, g * 256 : (g + 1) * 256] += bias_total
        col_sums[0:1, g * 128 : (g + 1) * 128] += col_total[0]
        col_sums[1:2, g * 128 : (g + 1) * 128] += col_total[1]


def attention_backward(branch, wproj, qkv, probs):
    rows, width = branch.shape
    windows = probs.shape[0]
    cols = qkv.shape[1]
    groups = cols // 384
    heads = groups * GROUP
    batch = batch_of(windows)
    quad_rows = batch * PAD
    return pl.pallas_call(
        functools.partial(bwd_kernel, groups),
        grid=(windows // batch,),
        in_specs=[
            whole((rows, width)),
            whole((heads * HEAD_DIM, width)),
            pl.BlockSpec((quad_rows, cols), lambda i: (i, 0)),
            pl.BlockSpec((batch, PAD, heads * PAD), lambda i: (i, 0, 0)),
        ],
        out_specs=[
            pl.BlockSpec((quad_rows, cols), lambda i: (i, 0)),
            whole((KEYS, heads * PAD)),
            whole((2, heads * HEAD_DIM)),
        ],
        out_shape=(
            jax.ShapeDtypeStruct((windows * PAD, cols), bf16),
            jax.ShapeDtypeStruct((KEYS, heads * PAD), f32),
            jax.ShapeDtypeStruct((2, heads * HEAD_DIM), f32),
        ),
        scratch_shapes=[pltpu.VMEM((rows + SPARE, width), f32), pltpu.VMEM((quad_rows, width), bf16)],
        compiler_params=params(),
        cost_estimate=pl.CostEstimate(
            flops=2 * windows * PAD * width * heads * 32 + 32 * windows * groups * 256 * 256 * 64,
            bytes_accessed=windows * PAD * cols * 6,
            transcendentals=0,
        ),
        name="attention_backward",
    )(branch, wproj, qkv, probs)


def input_kernel(parts, *refs):
    gqkvs, ws = refs[:parts], refs[parts : 2 * parts]
    tokens, grad_middle, gain, grad_tokens, sums, compact = refs[2 * parts :]
    step = pl.program_id(0)
    total = dot(gqkvs[0][...], ws[0][...], NT)
    for a, w in zip(gqkvs[1:], ws[1:]):
        total = total + dot(a[...], w[...], NT)
    batch = total.shape[0] // PAD
    view = step_rows(compact, step, batch)
    for j in range(batch):
        view[j * SLOTS : j * SLOTS + KEYS, :] = total[j * PAD : j * PAD + KEYS]

    @pl.when(step == pl.num_programs(0) - 1)
    def _():
        rows = tokens.shape[0]
        windows = pl.num_programs(0) * batch
        s_gain = s_shift = jnp.zeros((1, tokens.shape[1]), f32)
        for start, size in row_blocks(rows):
            at = slice(start, start + size)
            one = compact[at, :]
            if start + size == rows:
                real = start + lax.broadcasted_iota(jnp.int32, one.shape, 0) < windows * SLOTS
                one = jnp.where(real, one, 0.0)
            grad, for_gain = norm_back(tokens[at, :].astype(f32), gain[...], one)
            grad_tokens[at, :] = (grad_middle[at, :] + grad).astype(bf16)
            s_gain += col_sum(for_gain)
            s_shift += col_sum(one)
        sums[...] = jnp.concatenate([s_gain, s_shift], axis=0)


def input_backward(gqkvs, ws, tokens, grad_middle, gain):
    rows, width = tokens.shape
    quad_rows = batch_of(gqkvs[0].shape[0] // PAD) * PAD
    steps = gqkvs[0].shape[0] // quad_rows
    return pl.pallas_call(
        functools.partial(input_kernel, len(ws)),
        grid=(steps,),
        in_specs=[pl.BlockSpec((quad_rows, a.shape[1]), lambda i: (i, 0)) for a in gqkvs]
        + [whole(w.shape) for w in ws]
        + [whole((rows, width)), whole((rows, width)), whole((1, width))],
        out_specs=[whole((rows, width)), whole((2, width))],
        out_shape=(jax.ShapeDtypeStruct((rows, width), bf16), jax.ShapeDtypeStruct((2, width), f32)),
        scratch_shapes=[pltpu.VMEM((rows + SPARE, width), f32)],
        compiler_params=params(),
        cost_estimate=pl.CostEstimate(
            flops=2 * gqkvs[0].shape[0] * width * sum(w.shape[1] for w in ws), bytes_accessed=rows * width * 10, transcendentals=0
        ),
        name="input_backward",
    )(*gqkvs, *ws, tokens, grad_middle, gain)


def weight_kernel(adds, idx, left, right, *refs):
    value = dot(left[...], right[...], TN)
    for ref in refs[:adds]:
        value = value + ref[...].astype(f32)
    refs[adds][...] = value.astype(refs[adds].dtype)


def weight_split_kernel(relative, idx, left, right, near, far, send, keep, total):
    half = keep.shape[0]
    here = idx[2]
    total[...] = dot(left[...], right[...], TN) + near[...].astype(f32)
    for out, place, at in ((send, 1 - here, 1), (keep, here, 0)):
        rows = pl.ds(pl.multiple_of(place * half, 16), half)
        if relative:
            came = far[at * half : (at + 1) * half, :]
        else:
            came = far[rows, :]
        out[...] = (total[rows, :] + came.astype(f32)).astype(bf16)


def weight_grad(idx, left, left_width, right, right_width, adds=(), split=None, dtype=bf16):
    rows = left.shape[0]
    out = (left_width, right_width)
    step = left_width // 2 if split is None and left_width % 256 == 0 else left_width
    in_specs = [
        pl.BlockSpec((rows, step), lambda i, s: (0, s[0] * (left_width // step) + i)),
        pl.BlockSpec((rows, right_width), lambda i, s: (0, s[1])),
    ] + [pl.BlockSpec((step, right_width), lambda i, s: (i, 0)) for _ in adds]
    scratch = []
    if split is None:
        kernel = functools.partial(weight_kernel, len(adds))
        out_shape = jax.ShapeDtypeStruct(out, dtype)
        out_specs = pl.BlockSpec((step, right_width), lambda i, s: (i, 0))
    else:
        kernel = functools.partial(weight_split_kernel, split == "relative")
        half = (left_width // 2, right_width)
        out_shape = (jax.ShapeDtypeStruct(half, bf16),) * 2
        out_specs = [whole(half)] * 2
        scratch = [pltpu.VMEM(out, f32)]
    return pl.pallas_call(
        kernel,
        grid_spec=pltpu.PrefetchScalarGridSpec(
            num_scalar_prefetch=1, grid=(left_width // step,), in_specs=in_specs, out_specs=out_specs, scratch_shapes=scratch
        ),
        out_shape=out_shape,
        compiler_params=params(),
        cost_estimate=pl.CostEstimate(
            flops=2 * rows * left_width * right_width, bytes_accessed=2 * rows * (left_width + right_width), transcendentals=0
        ),
        name="weight_grad",
    )(idx, left, right, *adds)


def group_order():
    at = lax.broadcasted_iota(jnp.int32, (384, 384), 1)
    source = (at % 128) // 32 * 96 + at // 128 * 32 + at % 32
    return (lax.broadcasted_iota(jnp.int32, (384, 384), 0) == source).astype(f32).astype(bf16)


def as_given(piece):
    return piece.astype(f32)


def turned(piece):
    return piece.astype(f32).T


def head_order(piece):
    order = group_order()
    groups = [dot(piece[:, g : g + 384], order, NT) for g in range(0, piece.shape[1], 384)]
    return jnp.concatenate(groups, axis=1)


def place_kernel(change, places, *refs):
    step = pl.program_id(0)
    for i, ref in enumerate(refs[:-1]):

        @pl.when(step == i)
        def _(ref=ref):
            refs[-1][...] = change(ref[...])


def place(places, pieces, shape, change=as_given):
    if change is turned:
        block = pieces[0].shape[::-1]
    else:
        block = pieces[0].shape
    return pl.pallas_call(
        functools.partial(place_kernel, change),
        grid_spec=pltpu.PrefetchScalarGridSpec(
            num_scalar_prefetch=1,
            grid=(len(pieces),),
            in_specs=[whole(p.shape) for p in pieces],
            out_specs=pl.BlockSpec(block, lambda i, s: (s[2 * i], s[2 * i + 1])),
        ),
        out_shape=jax.ShapeDtypeStruct(shape, f32),
        compiler_params=params(),
        cost_estimate=pl.CostEstimate(flops=0, bytes_accessed=shape[0] * shape[1] * 6, transcendentals=0),
        name="place",
    )(places, *pieces)


def gather_kernel(places, *refs):
    pieces, out, sems = refs[:-2], refs[-2], refs[-1]
    rows = pieces[0].shape[0]
    copies = []
    for i, piece in enumerate(pieces):
        start = pl.multiple_of(places[i] * rows, 16)
        copies.append(pltpu.make_async_copy(piece, out.at[pl.ds(start, rows)], sems.at[i]))
    for copy in copies:
        copy.start()
    for copy in copies:
        copy.wait()


def gather_rows(places, pieces):
    rows, cols = pieces[0].shape
    return pl.pallas_call(
        gather_kernel,
        grid_spec=pltpu.PrefetchScalarGridSpec(
            num_scalar_prefetch=1,
            grid=(1,),
            in_specs=[pl.BlockSpec(memory_space=pl.ANY)] * len(pieces),
            out_specs=pl.BlockSpec(memory_space=pl.ANY),
            scratch_shapes=[pltpu.SemaphoreType.DMA((len(pieces),))],
        ),
        out_shape=jax.ShapeDtypeStruct((rows * len(pieces), cols), pieces[0].dtype),
        cost_estimate=pl.CostEstimate(flops=0, bytes_accessed=rows * cols * 16, transcendentals=0),
        name="gather_rows",
    )(places, *pieces)


def pair_onehot(rel_index, table_rows):
    turned_index = jnp.pad(rel_index.T, ((0, KEYS - SLOTS), (0, PAD - SLOTS)), constant_values=-1)
    offsets = jnp.arange(table_rows, dtype=jnp.int32)
    return (turned_index[None] == offsets[:, None, None]).astype(bf16)


def position_rows(onehot, table):
    rows, heads = table.shape
    flat = dot(onehot.reshape(rows, KEYS * PAD), table, TN)
    value = jnp.transpose(flat.reshape(KEYS, PAD, heads), (0, 2, 1)).reshape(KEYS, heads * PAD)
    return jnp.where(jnp.arange(KEYS)[:, None] < SLOTS, value, 2 * mask_fill)


def table_grad(onehot, sums):
    rows = onehot.shape[0]
    heads = sums.shape[1] // PAD
    flat = jnp.transpose(sums.reshape(KEYS, heads, PAD), (0, 2, 1)).reshape(KEYS * PAD, heads)
    high = flat.astype(bf16)
    rest = (flat - high.astype(f32)).astype(bf16)
    low = (flat - high.astype(f32) - rest.astype(f32)).astype(bf16)
    both = dot(onehot.reshape(rows, KEYS * PAD), jnp.concatenate([high, rest, low], axis=1))
    return both[:, :heads] + both[:, heads : 2 * heads] + both[:, 2 * heads :]


def window_mask(labels):
    shaped = labels.reshape(-1, SLOTS)
    keys = jnp.pad(shaped, ((0, 0), (0, KEYS - SLOTS)), constant_values=-2)[:, :, None]
    queries = jnp.pad(shaped, ((0, 0), (0, PAD - SLOTS)), constant_values=-3)
    queries = jnp.concatenate([queries, queries], axis=1)[:, None, :]
    key_at = jnp.arange(KEYS)[None, :, None]
    query_at = (jnp.arange(128) % PAD)[None, None, :]
    allowed = (keys == queries) & ((keys >= 0) | (key_at == query_at))
    outside = (key_at >= SLOTS) | (query_at >= SLOTS)
    return (allowed | outside).astype(f32)


def qkv_bias_row(bias_query, bias_value):
    groups = bias_query.shape[0] // 128
    query = bias_query.astype(f32).reshape(groups, 128)
    value = bias_value.astype(f32).reshape(groups, 128)
    return jnp.stack([query, jnp.zeros_like(query), value], axis=1).reshape(1, -1)


def row(vector):
    return vector.astype(f32).reshape(1, -1)


class Links:
    def __init__(self):
        at = lax.axis_index("dp")
        self.core = at % 2
        self.x = at // 2 % 2
        self.z = at // 4
        self.inner = (self.z == 1) | (self.z == 2)

    def y_swap(self, value):
        return lax.ppermute(value, "mp", [(0, 1), (1, 0)])

    def flip(self, value, bit):
        return lax.ppermute(value, "dp", [(i, i ^ bit) for i in range(16)])

    def core_swap(self, value):
        return self.flip(value, 1)

    def x_swap(self, value):
        return self.flip(value, 2)

    def z_pairs(self, value):
        return self.flip(value, 4)

    def z_move(self, value, pairs):
        return lax.ppermute(value, "dp", [(s * 4 + i, d * 4 + i) for s, d in pairs for i in range(4)])

    def z_sum(self, value):
        value = value + self.z_move(value, [(0, 1), (3, 2)])
        value = value + self.z_move(value, [(1, 2), (2, 1)])
        return jnp.where(self.inner, value, self.z_move(value, [(1, 0), (2, 3)]))

    def order(self):
        places = [2 * (self.core ^ (r >> 1)) + (self.x ^ (r & 1)) for r in range(4)]
        return jnp.stack(places).astype(jnp.int32)


def index_of(*items):
    return jnp.stack([jnp.asarray(i, jnp.int32) for i in items])


def step_grads(links, family):
    first = family("rem", False, (), None)
    second = family("rem", True, (links.core_swap(first),), None)
    far = links.y_swap(second)
    third = family("loc", False, (), None)
    send, keep = family("loc", True, (links.core_swap(third), far), True)
    piece = links.z_sum(keep + links.x_swap(send))
    beside = links.x_swap(piece)
    return [piece, beside, links.core_swap(piece), links.core_swap(beside)]


def on_device(
    direct,
    tokens,
    image_ids,
    rel_index,
    gain_one,
    shift_one,
    w_qkv,
    bias_query,
    bias_value,
    bias_table,
    w_proj,
    bias_proj,
    gain_two,
    shift_two,
    w_up,
    bias_up,
    w_down,
    bias_down,
    cotangent,
):
    mp = lax.axis_index("mp")
    real_rows = tokens.shape[0]
    labels = lax.dynamic_slice(image_ids, (mp * real_rows,), (real_rows,))
    spare = -real_rows % 16
    tokens = jnp.pad(tokens, ((0, spare), (0, 0)))
    cotangent = jnp.pad(cotangent, ((0, spare), (0, 0)))
    width = tokens.shape[1]
    table_rows = bias_table.shape[0]
    onehot = pair_onehot(rel_index, table_rows)
    mask = window_mask(labels)
    zero = jnp.zeros((), jnp.int32)

    local = (w_qkv, bias_query, bias_value, bias_table, w_proj, w_up.T, bias_up, w_down)
    if direct:
        links = Links()
        core, x = links.core, links.x
        order = links.order()
        heads_cols = bias_query.shape[0]
        units = bias_up.shape[0]
        small = jnp.concatenate([bias_query, bias_value, bias_up, bias_table.reshape(-1)])
        small = links.y_swap(small)
        query_rem = small[:heads_cols]
        value_rem = small[heads_cols : 2 * heads_cols]
        up_bias_rem = small[2 * heads_cols : 2 * heads_cols + units]
        table_rem = small[2 * heads_cols + units :].reshape(bias_table.shape)

        def fetch(weight):
            rows = weight.shape[0] // 4
            piece = lax.dynamic_slice(weight, (order[0] * rows, 0), (rows, weight.shape[1]))
            piece = links.y_swap(piece)
            beside = links.x_swap(piece)
            return gather_rows(order, (piece, beside, links.core_swap(piece), links.core_swap(beside)))

        qkv_rem = fetch(w_qkv)
        proj_rem = fetch(w_proj)
        piece_rows = units // 4
        own = [lax.dynamic_slice(w, (order[0] * piece_rows, 0), (piece_rows, width)) for w in (local[5], w_down)]
        even = links.z % 2 == 0
        came = links.y_swap(jnp.where(even, own[0], own[1]))
        swapped = links.z_pairs(came)
        both = []
        for piece in (jnp.where(even, came, swapped), jnp.where(even, swapped, came)):
            beside = links.x_swap(piece)
            both.append(jnp.concatenate([piece, beside, links.core_swap(piece), links.core_swap(beside)], axis=0))
        remote = (qkv_rem, query_rem, value_rem, table_rem, proj_rem, both[0], up_bias_rem, both[1])
        names = ("loc", "rem")
        parts = dict(loc=local, rem=remote)
        orders = dict(loc=jnp.arange(4, dtype=jnp.int32), rem=order)
    else:
        axes = (1, 0, 0, 1, 0, 0, 0, 0)
        names = ("all",)
        parts = dict(all=tuple(lax.all_gather(w, "mp", axis=a, tiled=True) for w, a in zip(local, axes)))
        orders = dict(all=jnp.arange(parts["all"][6].shape[0] // 384, dtype=jnp.int32))

    gain_first, shift_first = row(gain_one), row(shift_one)
    gain_second = row(gain_two)
    qkv, probs, att, w_in, pos = {}, {}, {}, {}, {}
    for name in names:
        w, b_query, b_value, table = parts[name][:4]
        qkv[name], probs[name], att[name], w_in[name], normed = attention_forward(
            tokens, gain_first, shift_first, w, qkv_bias_row(b_query, b_value), position_rows(onehot, table), mask
        )
    w_projs = {n: parts[n][4] for n in names}
    middle, low_two = project(
        [att[n] for n in names], [w_projs[n] for n in names], tokens, row(bias_proj), gain_second, row(shift_two)
    )
    hidden, gpre, up_bias_grad = {}, {}, {}
    carried = None
    for i, name in enumerate(reversed(names)):
        w_up_t, b_up, w_dn = parts[name][5:]
        finish = (middle, row(bias_down), gain_second) if i == len(names) - 1 else None
        bias = b_up.astype(f32).reshape(-1, 1, 384)
        got = mlp(orders[name], low_two, cotangent, w_up_t, bias, w_dn, carried, finish)
        hidden[name], gpre[name], up_bias_grad[name] = got[:3]
        carried = got[3:5]
    block_out, grad_middle, branch, sums_two = got[3:7]

    gqkv, bias_sums, col_sums = {}, {}, {}
    for name in reversed(names):
        gqkv[name], bias_sums[name], col_sums[name] = attention_backward(branch, w_projs[name], qkv[name], probs[name])
    grad_tokens, sums_one = input_backward(
        [gqkv[n] for n in names], [w_in[n] for n in names], tokens, grad_middle, gain_first
    )
    table_sums = {n: table_grad(onehot, bias_sums[n]) for n in names}

    if direct:

        def down_family(part, mine, adds, split):
            block = (0 if mine else 1) if part == "rem" else (core if mine else 1 - core)
            return weight_grad(
                index_of(block, 0, x), hidden[part], units // 2, cotangent, width, adds, "relative" if split else None
            )

        def up_family(part, mine, adds, split):
            block = (0 if mine else 1) if part == "rem" else (core if mine else 1 - core)
            return weight_grad(
                index_of(block, 0, x), gpre[part], units // 2, low_two, width, adds, "relative" if split else None
            )

        def proj_family(part, mine, adds, split):
            block = core if mine else 1 - core
            return weight_grad(
                index_of(0, block, x), att[part], att[part].shape[1], branch, width // 2, adds, "natural" if split else None
            )

        def qkv_family(part, mine, adds, split):
            block = core if mine else 1 - core
            return weight_grad(
                index_of(block, 0, x), normed, width // 2, gqkv[part], gqkv[part].shape[1], adds, "natural" if split else None
            )

        row_places = jnp.stack([order, jnp.zeros_like(order)], axis=1).reshape(-1)
        col_places = jnp.stack([jnp.zeros_like(order), order], axis=1).reshape(-1)
        proj_places = jnp.stack([order % 2, order // 2], axis=1).reshape(-1)
        grad_down = place(row_places, step_grads(links, down_family), w_down.shape)
        grad_up = place(col_places, step_grads(links, up_family), w_up.shape, turned)
        grad_proj = place(proj_places, step_grads(links, proj_family), w_proj.shape)
        grad_qkv = place(row_places, step_grads(links, qkv_family), w_qkv.shape, head_order)

        def reduce_small(shared, loc, rem):
            value = jnp.concatenate([shared, loc, rem])
            value = value + links.core_swap(value)
            value = value + links.x_swap(value)
            value = links.z_sum(value)
            n, m = shared.shape[0], loc.shape[0]
            far = links.y_swap(jnp.concatenate([value[:n], value[n + m :]]))
            return value[: n + m] + far

        def flat(name):
            return [col_sums[name].reshape(-1), up_bias_grad[name].reshape(-1), table_sums[name].reshape(-1)]

        shared = sums_two.reshape(-1)
        early = reduce_small(shared, jnp.concatenate(flat("loc")), jnp.concatenate(flat("rem")))
        late = reduce_small(sums_one.reshape(-1), jnp.zeros((0,), f32), jnp.zeros((0,), f32)).reshape(2, width)
        two = early[: 4 * width].reshape(4, width)
        early = early[4 * width :]
        grad_query_b, grad_value_b = early[:heads_cols], early[heads_cols : 2 * heads_cols]
        grad_up_bias = early[2 * heads_cols : 2 * heads_cols + units]
        grad_table = early[2 * heads_cols + units :].reshape(bias_table.shape)
    else:
        none = index_of(0, 0, 0)

        def summed(value, axis):
            value = lax.psum_scatter(value, "mp", scatter_dimension=axis, tiled=True)
            return lax.psum(value, "dp")

        def wide(value, axis):
            return summed(value.astype(bf16), axis).astype(f32)

        def full(left, right):
            return weight_grad(none, left, left.shape[1], right, right.shape[1])

        h, g, q = hidden["all"], gpre["all"], gqkv["all"]
        grad_down = wide(full(h, cotangent), 0)
        grad_up = wide(full(g, low_two).T, 1)
        grad_proj = wide(full(att["all"], branch), 0)
        by_group = full(normed, q).reshape(width, -1, 384)
        natural = dot(by_group.reshape(-1, 384), group_order(), NT).reshape(width, -1)
        grad_qkv = wide(natural, 1)
        grad_query_b = summed(col_sums["all"][0], 0)
        grad_value_b = summed(col_sums["all"][1], 0)
        grad_up_bias = summed(up_bias_grad["all"].reshape(-1), 0)
        grad_table = summed(table_sums["all"], 1)
        two, late = lax.psum((sums_two, sums_one), ("dp", "mp"))
    return (
        block_out[:real_rows],
        grad_tokens[:real_rows],
        late[0],
        late[1],
        grad_qkv,
        grad_query_b,
        grad_value_b,
        grad_table,
        grad_proj,
        two[2],
        two[0],
        two[1],
        grad_up,
        grad_up_bias,
        grad_down,
        two[3],
    )


def solution(mesh):
    direct = mesh.shape["dp"] == 16 and mesh.shape["mp"] == 2
    return jax.shard_map(
        functools.partial(on_device, direct),
        mesh=mesh,
        in_specs=(
            P(("dp", "mp"), None),
            P("dp"),
            P(),
            P(),
            P(),
            P(None, "mp"),
            P("mp"),
            P("mp"),
            P(None, "mp"),
            P("mp", None),
            P(),
            P(),
            P(),
            P(None, "mp"),
            P("mp"),
            P("mp", None),
            P(),
            P(("dp", "mp"), None),
        ),
        out_specs=(
            P(("dp", "mp"), None),
            P(("dp", "mp"), None),
            P(),
            P(),
            P(None, "mp"),
            P("mp"),
            P("mp"),
            P(None, "mp"),
            P("mp", None),
            P(),
            P(),
            P(),
            P(None, "mp"),
            P("mp"),
            P("mp", None),
            P(),
        ),
        check_vma=False,
    )
```

time: 816 us -> 530 us (0.65)
  Pallas kernels: 0 us -> 274 us
  waiting for transfers between devices: 312 us -> 96.2 us
  local copies, waits for them, and re-layouts: 175 us -> 42.9 us
  matrix products: 131 us -> 6.96 us
  blocking collectives: 102 us -> 0 us
  starting transfers between devices: 0.99 us -> 67.7 us
  other arithmetic: 69.7 us -> 31.3 us
  between operations: 14.5 us -> 2.19 us
    pallas_call x0 -> x30, Pallas kernels: none -> 274 us  [the longest x2 75.1 us: gather_rows(): pl.pallas_call(gather_kernel, grid_spec=pltpu.PrefetchScalarGridSpec(num_...]
    reduce_scatter x4 -> x0, waiting for transfers between devices: 173 us -> none  [the longest x1 60.5 us: on_device(): lax.psum_scatter(jnp.dot(attended, proj_use, preferred_element_type=jnp.f...]
    dot_general x28 -> x4, matrix products: 131 us -> 6.96 us  [dot(): lax.dot_general(left, right, (dims, ((), ())), preferred_element_type=f32)]
    all_gather x4 -> x0, waiting for transfers between devices: 104 us -> none  [the longest x1 37.2 us: on_device(): rows_one = lax.all_gather(low_one, 'mp', axis=0, tiled=True)]
    psum x2 -> x0, blocking collectives: 102 us -> none  [the longest x1 62.1 us: on_device(): lax.psum(grad_query_b.astype(jnp.bfloat16), 'dp').astype(jnp.float32)]
    ppermute x0 -> x69, waiting for transfers between devices: none -> 96.2 us  [the longest x41 42.9 us: flip(): return lax.ppermute(value, 'dp', [(i, i ^ bit) for i in range(16)])]
    convert_element_type x7 -> x3, local copies, waits for them, and re-layouts: 76.8 us -> 0.63 us  [the longest x1 0.6 us: on_device(): bias = b_up.astype(f32).reshape(-1, 1, 384)]
    ppermute x0 -> x69, starting transfers between devices: none -> 67.7 us  [the longest x18 31.5 us: z_move(): lax.ppermute(value, 'dp', [(s * 4 + i, d * 4 + i) for s, d in pairs for i...]
  transfers between devices with their start and end apart: 9 -> 69, of which waited for: 9 -> 15; matrix products, arithmetic and copies ran while one was open for 15% -> 13% of each run, Pallas kernels for 0% -> 47%
where the time goes in v1:
time: 530 us; the launch traced here: 522 us
  Pallas kernels  274 us (52%)
  waiting for transfers between devices  96.2 us (18%)
  starting transfers between devices  67.7 us (13%)
  local copies, waits for them, and re-layouts  42.9 us (8%)
  other arithmetic  31.3 us (6%)
  matrix products  6.96 us (1%)
    pallas_call x2, Pallas kernels, gather_rows(): pl.pallas_call(gather_kernel, grid_spec=pltpu.PrefetchScalarGridSpec(num_...  75.1 us
    pallas_call x16, Pallas kernels, weight_grad(): pl.pallas_call(kernel, grid_spec=pltpu.PrefetchScalarGridSpec(num_scalar_...  72.9 us
    ppermute x41, waiting for transfers between devices, flip(): return lax.ppermute(value, 'dp', [(i, i ^ bit) for i in range(16)])  42.9 us
    ppermute x18, waiting for transfers between devices, z_move(): lax.ppermute(value, 'dp', [(s * 4 + i, d * 4 + i) for s, d in pairs for i...  41.5 us
    pallas_call x2, Pallas kernels, mlp(): pl.pallas_call(functools.partial(mlp_kernel, first, last), grid_spec=pltp...  41.4 us
    ppermute x18, starting transfers between devices, z_move(): lax.ppermute(value, 'dp', [(s * 4 + i, d * 4 + i) for s, d in pairs for i...  31.5 us
    pallas_call x2, Pallas kernels, attention_backward(): pl.pallas_call(functools.partial(bwd_kernel, groups), grid=(windows // ba...  26.1 us
    ppermute x41, starting transfers between devices, flip(): return lax.ppermute(value, 'dp', [(i, i ^ bit) for i in range(16)])  23.9 us
  transfers between devices with their start and end apart: 69, of which 15 were waited for; matrix products, arithmetic and copies ran while one was open for 13% of the time, Pallas kernels for 47%

profile of v1, /device:TPU:0, one launch (start us, length us, event | category | flops | bytes accessed | tf_op | source)
XLA Modules:
  0.0 521.5 jit_solution(11958080626426816643)
XLA Ops:
  0.7 2.8 copy.58
  3.6 1.7 bitcast_select_fusion
  5.3 3.0 collective-permute-start.9
  8.4 1.6 constant_dynamic-slice_fusion
  10.0 1.8 constant_dynamic-slice_fusion.1
  11.8 2.0 collective-permute-start
  27.6 1.8 or_convert_fusion.mask
  29.4 2.5 fusion.10
  46.8 2.1 collective-permute-start.10
  48.9 2.7 fusion.11
  55.4 5.8 %collective-permute-done.10 = bf16[384,768]{1,0:T(8,128)(2,1)S(1)} collective-permute-done((bf16[384,768]{1,0:T(8,128)(2,1)S(1)}, bf16[384,768]{1,0:T(8,128)(2,1)S(1)}, u32[]{:S(2)}, u32[]{:S(2)}) %collective-permute-start.10) | collective-permute-done | bytes 589856 | tf_op jit(solution)/shard_map/ppermute | solution.py:684
  61.2 1.7 collective-permute-start.14
  64.2 4.7 collective-permute-done.1.refs_1_
  69.5 2.4 collective-permute-start.11
  72.0 11.5 %attention_forward.2 = (bf16[1024,1152]{1,0:T(8,128)(2,1)}, bf16[16,64,768]{2,1,0:T(8,128)(2,1)}, bf16[784,384]{1,0:T(8,128)(2,1)}, bf16[768,1152]{1,0:T(8,128)(2,1)}, bf16[1024,768]{1,0:T(8,128)(2,1)}) custom-call(bf16[784,768]{1,0:T(8,128)(2,1)} %refs_4_.5, f32[1,768]{1,0:T(1,128)} %reshape.716.gain.refs_6_, f32[1,768]{1,0:T(1,128)} %reshape.718.shift, ...), custom_call_target="tpu_custom_call" | custom-call | flops 5033164800 | bytes 8257536 | tf_op jit(solution)/shard_map/attention_forward/pallas_call | solution.py:174
  85.9 19.7 %gather_rows.3.refs_3_.wproj = bf16[384,768]{1,0:T(8,128)(2,1)} custom-call(s32[4]{0:T(128)} %pad_add_fusion.7.places.order, bf16[96,768]{1,0:T(8,128)(2,1)} %collective-permute-done.5.refs_0_, bf16[96,768]{1,0:T(8,128)(2,1)} %copy-done.25, bf16[96,768]{1,0:T(8,128)(2,1)} %copy-done.26, bf16[96,768]{1,0:T(8,128)(2,1)} %collective-permute-done.8.refs_3_), custom_call_target="tpu_custom_call" | custom-call | bytes 1179648 | tf_op jit(solution)/shard_map/gather_rows/pallas_call | solution.py:610
  105.9 55.4 %gather_rows.2.w = bf16[768,1152]{1,0:T(8,128)(2,1)} custom-call(s32[4]{0:T(128)} %pad_add_fusion.7.places.order, bf16[192,1152]{1,0:T(8,128)(2,1)} %collective-permute-done.refs_0_, bf16[192,1152]{1,0:T(8,128)(2,1)} %collective-permute-done.1.refs_1_, bf16[192,1152]{1,0:T(8,128)(2,1)} %collective-permute-done.2.refs_2_, ...), custom_call_target="tpu_custom_call" | custom-call | bytes 3538944 | tf_op jit(solution)/shard_map/gather_rows/pallas_call | solution.py:610
  161.7 11.7 %attention_forward.3 = (bf16[1024,1152]{1,0:T(8,128)(2,1)}, bf16[16,64,768]{2,1,0:T(8,128)(2,1)}, bf16[784,384]{1,0:T(8,128)(2,1)}, bf16[768,1152]{1,0:T(8,128)(2,1)}, bf16[1024,768]{1,0:T(8,128)(2,1)}) custom-call(bf16[784,768]{1,0:T(8,128)(2,1)} %refs_4_.5, f32[1,768]{1,0:T(1,128)} %reshape.716.gain.refs_6_, f32[1,768]{1,0:T(1,128)} %reshape.718.shift, ...), custom_call_target="tpu_custom_call" | custom-call | flops 5033164800 | bytes 8257536 | tf_op jit(solution)/shard_map/attention_forward/pallas_call | solution.py:174
  173.4 5.3 %project.1 = (f32[784,768]{1,0:T(8,128)}, bf16[784,768]{1,0:T(8,128)(2,1)}) custom-call(bf16[784,384]{1,0:T(8,128)(2,1)} %get-tuple-element.55.refs_0_.left, bf16[784,384]{1,0:T(8,128)(2,1)} %get-tuple-element.56.refs_1_.left, bf16[384,768]{1,0:T(8,128)(2,1)} %wproj.1, bf16[384,768]{1,0:T(8,128)(2,1)} %gather_rows.3.refs_3_.wproj, bf16[784,768]{1,0:T(8,128)(2,1)} %refs_4_.5, ...), custom_call_target="tpu_custom_call" | custom-call | flops 924844032 | bytes 6021120 | tf_op jit(solution)/shard_map/project/pallas_call | solution.py:223
  178.7 1.6 pad_maximum_fusion.1.refs_4_
  180.3 5.6 %pad_maximum_fusion.refs_2_ = bf16[1536,768]{1,0:T(8,128)(2,1)} fusion(bf16[384,768]{1,0:T(8,128)(2,1)S(1)} %collective-permute-done.13, bf16[384,768]{1,0:T(8,128)(2,1)} %collective-permute-done.12, bf16[384,768]{1,0:T(8,128)(2,1)S(1)} %collective-permute-done.11, bf16[384,768]{1,0:T(8,128)(2,1)S(1)} %get-tuple-element.129), kind=kLoop, calls=%fused_computation.8 | loop fusion | flops 9437184 | bytes 4718592 | tf_op jit(solution)/shard_map/concatenate | solution.py:787
  185.9 18.2 %mlp.2 = (bf16[784,1536]{1,0:T(8,128)(2,1)}, bf16[784,1536]{1,0:T(8,128)(2,1)}, f32[4,1,384]{2,1,0:T(1,128)}, f32[784,768]{1,0:T(8,128)}, f32[784,768]{1,0:T(8,128)}) custom-call(s32[4]{0:T(128)} %pad_add_fusion.7.places.order, bf16[784,768]{1,0:T(8,128)(2,1)} %get-tuple-element.57.refs_0_.right, bf16[784,768]{1,0:T(8,128)(2,1)} %right.7, ...), custom_call_target="tpu_custom_call" | custom-call | flops 7398752256 | bytes 4816896 | tf_op jit(solution)/shard_map/mlp/pallas_call | solution.py:345
  204.1 5.0 weight_grad.29
  210.0 23.2 %mlp.3 = (bf16[784,1536]{1,0:T(8,128)(2,1)}, bf16[784,1536]{1,0:T(8,128)(2,1)}, f32[4,1,384]{2,1,0:T(1,128)}, bf16[784,768]{1,0:T(8,128)(2,1)}, f32[784,768]{1,0...) custom-call(s32[4]{0:T(128)} %iota.38.order, bf16[784,768]{1,0:T(8,128)(2,1)} %get-tuple-element.57.refs_0_.right, ...), custom_call_target="tpu_custom_call" | custom-call | flops 7398752256 | bytes 4816896 | tf_op jit(solution)/shard_map/mlp/pallas_call | solution.py:345
  233.2 4.6 weight_grad.28
  238.1 4.6 weight_grad.25
  243.0 4.6 weight_grad.24
  247.9 13.0 %attention_backward.3 = (bf16[1024,1152]{1,0:T(8,128)(2,1)}, f32[56,768]{1,0:T(8,128)}, f32[2,384]{1,0:T(2,128)}) custom-call(bf16[784,768]{1,0:T(8,128)(2,1)} %get-tuple-element.62.branch.right, bf16[384,768]{1,0:T(8,128)(2,1)} %gather_rows.3.refs_3_.wproj, bf16[1024,1152]{1,0:T(8,128)(2,1)} %get-tuple-element.66.qkv, ...), custom_call_target="tpu_custom_call" | custom-call | flops 7046430720 | bytes 7077888 | tf_op jit(solution)/shard_map/attention_backward/pallas_call | solution.py:412
  260.9 13.2 %attention_backward.2 = (bf16[1024,1152]{1,0:T(8,128)(2,1)}, f32[56,768]{1,0:T(8,128)}, f32[2,384]{1,0:T(2,128)}) custom-call(bf16[784,768]{1,0:T(8,128)(2,1)} %get-tuple-element.62.branch.right, bf16[384,768]{1,0:T(8,128)(2,1)} %wproj.1, bf16[1024,1152]{1,0:T(8,128)(2,1)} %get-tuple-element.63.qkv, bf16[16,64,768]{2,1,0:T(8,128)(2,1)} %get-tuple-element.64.probs), custom_call_target="tpu_custom_call" | custom-call | flops 7046430720 | bytes 7077888 | tf_op jit(solution)/shard_map/attention_backward/pallas_call | solution.py:412
  275.7 4.7 weight_grad.17
  280.7 4.8 weight_grad.30
  287.1 4.8 weight_grad.26
  292.4 4.8 weight_grad.16
  297.2 11.2 %input_backward.1 = (bf16[784,768]{1,0:T(8,128)(2,1)}, f32[2,768]{1,0:T(2,128)}) custom-call(bf16[1024,1152]{1,0:T(8,128)(2,1)} %get-tuple-element.65.refs_0_.right, bf16[1024,1152]{1,0:T(8,128)(2,1)} %get-tuple-element.68.refs_1_.right, bf16[768,1152]{1,0:T(8,128)(2,1)} %get-tuple-element.69.refs_2_, bf16[768,1152]{1,0:T(8,128)(2,1)} %get-tuple-element.70.refs_3_, ...), custom_call_target="tpu_custom_call" | custom-call | flops 3623878656 | bytes 6021120 | tf_op jit(solution)/shard_map/input_backward/pallas_call | solution.py:476
  308.5 6.0 %collective-permute-done.61.far = bf16[768,768]{1,0:T(8,128)(2,1)S(1)} collective-permute-done((bf16[768,768]{1,0:T(8,128)(2,1)}, bf16[768,768]{1,0:T(8,128)(2,1)S(1)}, u32[]{:S(2)}, u32[]{:S(2)}) %collective-permute-start.61) | collective-permute-done | bytes 1179680 | tf_op jit(solution)/shard_map/ppermute | solution.py:681
  315.6 5.7 %weight_grad.31 = (bf16[384,768]{1,0:T(8,128)(2,1)}, bf16[384,768]{1,0:T(8,128)(2,1)}) custom-call(s32[3]{0:T(128)} %fusion.30.idx, bf16[784,1536]{1,0:T(8,128)(2,1)} %get-tuple-element.90.left, bf16[784,768]{1,0:T(8,128)(2,1)} %right.7, bf16[768,768]{1,0:T(8,128)(2,1)} %copy-done.5, bf16[768,768]{1,0:T(8,128)(2,1)} %copy-done.6), custom_call_target="tpu_custom_call" | custom-call | flops 924844032 | bytes 2408448 | tf_op jit(solution)/shard_map/weight_grad/pallas_call | solution.py:532
  322.5 4.9 weight_grad.18
  330.2 3.2 weight_grad.21
  334.1 5.8 %collective-permute-done.51.far = bf16[768,768]{1,0:T(8,128)(2,1)} collective-permute-done((bf16[768,768]{1,0:T(8,128)(2,1)}, bf16[768,768]{1,0:T(8,128)(2,1)}, u32[]{:S(2)}, u32[]{:S(2)}) %collective-permute-start.51) | collective-permute-done | bytes 1179680 | tf_op jit(solution)/shard_map/ppermute | solution.py:681
  339.9 5.7 %weight_grad.27 = (bf16[384,768]{1,0:T(8,128)(2,1)}, bf16[384,768]{1,0:T(8,128)(2,1)}) custom-call(s32[3]{0:T(128)} %fusion.30.idx, bf16[784,1536]{1,0:T(8,128)(2,1)} %get-tuple-element.86.left, bf16[784,768]{1,0:T(8,128)(2,1)} %get-tuple-element.57.refs_0_.right, bf16[768,768]{1,0:T(8,128)(2,1)} %copy-done.4, bf16[768,768]{1,0:T(8,128)(2,1)} %collective-permute-done.51.far), custom_call_target="tpu_custom_call" | custom-call | flops 924844032 | bytes 2408448 | tf_op jit(solution)/shard_map/weight_grad/pallas_call | solution.py:532
  347.7 2.5 collective-permute-start.63
  352.7 3.2 weight_grad.20
  358.2 3.3 weight_grad.22
  363.9 5.3 %weight_grad.19 = (bf16[192,1152]{1,0:T(8,128)(2,1)}, bf16[192,1152]{1,0:T(8,128)(2,1)}) custom-call(s32[3]{0:T(128)} %fusion.30.idx, bf16[1024,768]{1,0:T(8,128)(2,1)} %get-tuple-element.74.left, bf16[1024,1152]{1,0:T(8,128)(2,1)} %get-tuple-element.65.refs_0_.right, bf16[384,1152]{1,0:T(8,128)(2,1)} %collective-permute-done.23.near, ...), custom_call_target="tpu_custom_call" | custom-call | flops 905969664 | bytes 3145728 | tf_op jit(solution)/shard_map/weight_grad/pallas_call | solution.py:532
  369.5 1.8 collective-permute-start.34
  372.5 9.8 %collective-permute-done.34 = f32[11736]{0:T(1024)S(1)} collective-permute-done((f32[11736]{0:T(1024)S(1)}, f32[11736]{0:T(1024)S(1)}, u32[]{:S(2)}, u32[]{:S(2)}) %collective-permute-start.34) | collective-permute-done | bytes 46976 | tf_op jit(solution)/shard_map/ppermute | solution.py:684
  382.3 2.4 collective-permute-start.53
  387.5 3.4 weight_grad.23
  390.9 6.1 %collective-permute-done.19 = f32[1536]{0:T(1024)S(1)} collective-permute-done((f32[1536]{0:T(1024)S(1)}, f32[1536]{0:T(1024)S(1)}, u32[]{:S(2)}, u32[]{:S(2)}) %collective-permute-start.19) | collective-permute-done | bytes 6176 | tf_op jit(solution)/shard_map/ppermute | solution.py:696
  399.5 2.9 collective-permute-done.42
  404.0 10.6 %collective-permute-start.43 = (bf16[192,384]{1,0:T(8,128)(2,1)S(1)}, bf16[192,384]{1,0:T(8,128)(2,1)}, u32[]{:S(2)}, u32[]{:S(2)}) collective-permute-start(bf16[192,384]{1,0:T(8,128)(2,1)S(1)} %add.193), channel_id=1, source_target_pairs={{0,8},{2,10},{4,12},{6,14},{24,16},{26,18},{28,20},{30,22},{1,9},{... | collective-permute-start | bytes 442376 | tf_op jit(solution)/shard_map/ppermute | solution.py:696
  423.4 1.8 collective-permute-start.22
  430.6 10.0 %collective-permute-done.45 = bf16[192,384]{1,0:T(8,128)(2,1)S(1)} collective-permute-done((bf16[192,384]{1,0:T(8,128)(2,1)S(1)}, bf16[192,384]{1,0:T(8,128)(2,1)S(1)}, u32[]{:S(2)}, u32[]{:S(2)}) %collective-permute-start.45) | collective-permute-done | bytes 147488 | tf_op jit(solution)/shard_map/ppermute | solution.py:696
  440.9 1.8 collective-permute-start.46
  442.8 11.3 %collective-permute-done.65 = bf16[384,768]{1,0:T(8,128)(2,1)S(1)} collective-permute-done((bf16[384,768]{1,0:T(8,128)(2,1)S(1)}, bf16[384,768]{1,0:T(8,128)(2,1)S(1)}, u32[]{:S(2)}, u32[]{:S(2)}) %collective-permute-start.65) | collective-permute-done | bytes 589856 | tf_op jit(solution)/shard_map/ppermute | solution.py:696
  455.5 10.2 %collective-permute-done.55 = bf16[384,768]{1,0:T(8,128)(2,1)S(1)} collective-permute-done((bf16[384,768]{1,0:T(8,128)(2,1)S(1)}, bf16[384,768]{1,0:T(8,128)(2,1)S(1)}, u32[]{:S(2)}, u32[]{:S(2)}) %collective-permute-start.55) | collective-permute-done | bytes 589856 | tf_op jit(solution)/shard_map/ppermute | solution.py:696
  465.7 1.7 collective-permute-start.66
  467.5 3.0 collective-permute-done.29
  470.5 1.7 collective-permute-start.56
  477.0 18.9 %collective-permute-done.30.refs_1_ = bf16[192,1152]{1,0:T(8,128)(2,1)} collective-permute-done((bf16[192,1152]{1,0:T(8,128)(2,1)S(1)}, bf16[192,1152]{1,0:T(8,128)(2,1)}, u32[]{:S(2)}, u32[]{:S(2)}) %collective-permute-start.30) | collective-permute-done | bytes 442400 | tf_op jit(solution)/shard_map/ppermute | solution.py:684
  500.3 3.4 place.5
  504.5 5.6 %place.4 = f32[768,1152]{1,0:T(8,128)} custom-call(s32[8]{0:T(128)} %reshape.701.places, bf16[192,1152]{1,0:T(8,128)(2,1)} %copy-done.3, bf16[192,1152]{1,0:T(8,128)(2,1)} %collective-permute-done.30.refs_1_, bf16[192,1152]{1,0:T(8,128)(2,1)} %collective-permute-done.31.refs_2_, bf16[192,1152]{1,0:T(8,128)(2,1)} %copy-done.18), custom_call_target="tpu_custom_call" | custom-call | bytes 5308416 | tf_op jit(solution)/shard_map/place/pallas_call | solution.py:580
  510.2 4.9 place.7
  515.9 5.2 place.6
  (317 shorter events, 93.0 us)
Async XLA Ops:
  5.3 41.5 %collective-permute-start.9 = (bf16[384,768]{1,0:T(8,128)(2,1)S(1)}, bf16[384,768]{1,0:T(8,128)(2,1)S(1)}, u32[]{:S(2)}, u32[]{:S(2)}) collective-permute-start(bf16[384,768]{1,0:T(8,128)(2,1)S(1)} %bitcast_select_fusion), channel_id=1, source_target_pairs={{0,1},{1,0},{2,3},{3,2},{4,5},{5,4},{6,7},{7,6},{8,9},{9,8},{10,11... | collective-permute-start | bytes 1769480 | tf_op jit(solution)/shard_map/ppermute | solution.py:681
  9.9 43.4 %collective-permute-start.5 = (bf16[96,768]{1,0:T(8,128)(2,1)}, bf16[96,768]{1,0:T(8,128)(2,1)}, u32[]{:S(2)}, u32[]{:S(2)}) collective-permute-start(bf16[96,768]{1,0:T(8,128)(2,1)} %constant_dynamic-slice_fusion), channel_id=1, source_target_pairs={{0,1},{1,0},{2,3},{3,2},{4,5},{5,4},{6,7},{7,6},{8,9},{9,8},{10,11... | collective-permute-start | bytes 442376 | tf_op jit(solution)/shard_map/ppermute | solution.py:681
  11.8 43.1 %collective-permute-start = (bf16[192,1152]{1,0:T(8,128)(2,1)}, bf16[192,1152]{1,0:T(8,128)(2,1)}, u32[]{:S(2)}, u32[]{:S(2)}) collective-permute-start(bf16[192,1152]{1,0:T(8,128)(2,1)} %constant_dynamic-slice_fusion.1), channel_id=1, source_target_pairs={{0,1},{1,0},{2,3},{3,2},{4,5},{5,4},{6,7},{7,6},{8,9},{9,8},{10,11... | collective-permute-start | bytes 1327112 | tf_op jit(solution)/shard_map/ppermute | solution.py:681
  16.7 29.2 %collective-permute-start.4 = (bf16[4332]{0:T(1024)(128)(2,1)}, bf16[4332]{0:T(1024)(128)(2,1)}, u32[]{:S(2)}, u32[]{:S(2)}) collective-permute-start(bf16[4332]{0:T(1024)(128)(2,1)} %pad_maximum_fusion.3), channel_id=1, source_target_pairs={{0,1},{1,0},{2,3},{3,2},{4,5},{5,4},{6,7},{7,6},{8,9},{9,8},{10,11... | collective-permute-start | bytes 26000 | tf_op jit(solution)/shard_map/ppermute | solution.py:681
  46.8 14.3 %collective-permute-start.10 = (bf16[384,768]{1,0:T(8,128)(2,1)S(1)}, bf16[384,768]{1,0:T(8,128)(2,1)S(1)}, u32[]{:S(2)}, u32[]{:S(2)}) collective-permute-start(bf16[384,768]{1,0:T(8,128)(2,1)S(1)} %collective-permute-done.9), channel_id=1, source_target_pairs={{0,8},{2,10},{4,12},{6,14},{8,0},{10,2},{12,4},{14,6},{16,24},{18,... | collective-permute-start | bytes 1769480 | tf_op jit(solution)/shard_map/ppermute | solution.py:684
  53.4 10.3 %collective-permute-start.6 = (bf16[96,768]{1,0:T(8,128)(2,1)}, bf16[96,768]{1,0:T(8,128)(2,1)S(1)}, u32[]{:S(2)}, u32[]{:S(2)}) collective-permute-start(bf16[96,768]{1,0:T(8,128)(2,1)} %collective-permute-done.5.refs_0_), channel_id=1, source_target_pairs={{0,4},{2,6},{4,0},{6,2},{8,12},{10,14},{12,8},{14,10},{16,20},{18,... | collective-permute-start | bytes 442376 | tf_op jit(solution)/shard_map/ppermute | solution.py:684
  54.9 14.0 %collective-permute-start.7 = (bf16[96,768]{1,0:T(8,128)(2,1)}, bf16[96,768]{1,0:T(8,128)(2,1)S(1)}, u32[]{:S(2)}, u32[]{:S(2)}) collective-permute-start(bf16[96,768]{1,0:T(8,128)(2,1)} %collective-permute-done.5.refs_0_), channel_id=1, source_target_pairs={{0,2},{2,0},{4,6},{6,4},{8,10},{10,8},{12,14},{14,12},{16,18},{18,... | collective-permute-start | bytes 442376 | tf_op jit(solution)/shard_map/ppermute | solution.py:684
  54.9 14.0 %collective-permute-start.1 = (bf16[192,1152]{1,0:T(8,128)(2,1)}, bf16[192,1152]{1,0:T(8,128)(2,1)}, u32[]{:S(2)}, u32[]{:S(2)}) collective-permute-start(bf16[192,1152]{1,0:T(8,128)(2,1)} %collective-permute-done.refs_0_), channel_id=1, source_target_pairs={{0,4},{2,6},{4,0},{6,2},{8,12},{10,14},{12,8},{14,10},{16,20},{18,... | collective-permute-start | bytes 1327112 | tf_op jit(solution)/shard_map/ppermute | solution.py:684
  61.2 22.5 %collective-permute-start.14 = (bf16[384,768]{1,0:T(8,128)(2,1)S(1)}, bf16[384,768]{1,0:T(8,128)(2,1)S(1)}, u32[]{:S(2)}, u32[]{:S(2)}) collective-permute-start(bf16[384,768]{1,0:T(8,128)(2,1)S(1)} %get-tuple-element.128), channel_id=1, source_target_pairs={{0,4},{2,6},{4,0},{6,2},{8,12},{10,14},{12,8},{14,10},{16,20},{18,... | collective-permute-start | bytes 1769480 | tf_op jit(solution)/shard_map/ppermute | solution.py:684
  63.6 19.8 %collective-permute-start.8 = (bf16[96,768]{1,0:T(8,128)(2,1)S(1)}, bf16[96,768]{1,0:T(8,128)(2,1)}, u32[]{:S(2)}, u32[]{:S(2)}) collective-permute-start(bf16[96,768]{1,0:T(8,128)(2,1)S(1)} %collective-permute-done.6.refs_1_), channel_id=1, source_target_pairs={{0,2},{2,0},{4,6},{6,4},{8,10},{10,8},{12,14},{14,12},{16,18},{18,... | collective-permute-start | bytes 442376 | tf_op jit(solution)/shard_map/ppermute | solution.py:684
  63.7 42.0 %collective-permute-start.2 = (bf16[192,1152]{1,0:T(8,128)(2,1)}, bf16[192,1152]{1,0:T(8,128)(2,1)}, u32[]{:S(2)}, u32[]{:S(2)}) collective-permute-start(bf16[192,1152]{1,0:T(8,128)(2,1)} %collective-permute-done.refs_0_), channel_id=1, source_target_pairs={{0,2},{2,0},{4,6},{6,4},{8,10},{10,8},{12,14},{14,12},{16,18},{18,... | collective-permute-start | bytes 1327112 | tf_op jit(solution)/shard_map/ppermute | solution.py:684
  68.8 37.1 %collective-permute-start.3 = (bf16[192,1152]{1,0:T(8,128)(2,1)}, bf16[192,1152]{1,0:T(8,128)(2,1)}, u32[]{:S(2)}, u32[]{:S(2)}) collective-permute-start(bf16[192,1152]{1,0:T(8,128)(2,1)} %collective-permute-done.1.refs_1_), channel_id=1, source_target_pairs={{0,2},{2,0},{4,6},{6,4},{8,10},{10,8},{12,14},{14,12},{16,18},{18,... | collective-permute-start | bytes 1327112 | tf_op jit(solution)/shard_map/ppermute | solution.py:684
  69.5 91.8 %collective-permute-start.11 = (bf16[384,768]{1,0:T(8,128)(2,1)S(1)}, bf16[384,768]{1,0:T(8,128)(2,1)S(1)}, u32[]{:S(2)}, u32[]{:S(2)}) collective-permute-start(bf16[384,768]{1,0:T(8,128)(2,1)S(1)} %get-tuple-element.129), channel_id=1, source_target_pairs={{0,4},{2,6},{4,0},{6,2},{8,12},{10,14},{12,8},{14,10},{16,20},{18,... | collective-permute-start | bytes 1769480 | tf_op jit(solution)/shard_map/ppermute | solution.py:684
  83.4 95.2 %collective-permute-start.15 = (bf16[384,768]{1,0:T(8,128)(2,1)S(1)}, bf16[384,768]{1,0:T(8,128)(2,1)S(1)}, u32[]{:S(2)}, u32[]{:S(2)}) collective-permute-start(bf16[384,768]{1,0:T(8,128)(2,1)S(1)} %get-tuple-element.128), channel_id=1, source_target_pairs={{0,2},{2,0},{4,6},{6,4},{8,10},{10,8},{12,14},{14,12},{16,18},{18,... | collective-permute-start | bytes 1769480 | tf_op jit(solution)/shard_map/ppermute | solution.py:684
  83.7 94.9 %collective-permute-start.16 = (bf16[384,768]{1,0:T(8,128)(2,1)S(1)}, bf16[384,768]{1,0:T(8,128)(2,1)S(1)}, u32[]{:S(2)}, u32[]{:S(2)}) collective-permute-start(bf16[384,768]{1,0:T(8,128)(2,1)S(1)} %collective-permute-done.14), channel_id=1, source_target_pairs={{0,2},{2,0},{4,6},{6,4},{8,10},{10,8},{12,14},{14,12},{16,18},{18,... | collective-permute-start | bytes 1769480 | tf_op jit(solution)/shard_map/ppermute | solution.py:684
  105.6 74.7 %collective-permute-start.12 = (bf16[384,768]{1,0:T(8,128)(2,1)S(1)}, bf16[384,768]{1,0:T(8,128)(2,1)}, u32[]{:S(2)}, u32[]{:S(2)}) collective-permute-start(bf16[384,768]{1,0:T(8,128)(2,1)S(1)} %get-tuple-element.129), channel_id=1, source_target_pairs={{0,2},{2,0},{4,6},{6,4},{8,10},{10,8},{12,14},{14,12},{16,18},{18,... | collective-permute-start | bytes 1769480 | tf_op jit(solution)/shard_map/ppermute | solution.py:684
  161.3 19.0 %collective-permute-start.13 = (bf16[384,768]{1,0:T(8,128)(2,1)S(1)}, bf16[384,768]{1,0:T(8,128)(2,1)S(1)}, u32[]{:S(2)}, u32[]{:S(2)}) collective-permute-start(bf16[384,768]{1,0:T(8,128)(2,1)S(1)} %collective-permute-done.11), channel_id=1, source_target_pairs={{0,2},{2,0},{4,6},{6,4},{8,10},{10,8},{12,14},{14,12},{16,18},{18,... | collective-permute-start | bytes 1769480 | tf_op jit(solution)/shard_map/ppermute | solution.py:684
  209.2 71.5 %collective-permute-start.60 = (bf16[768,768]{1,0:T(8,128)(2,1)}, bf16[768,768]{1,0:T(8,128)(2,1)}, u32[]{:S(2)}, u32[]{:S(2)}) collective-permute-start(bf16[768,768]{1,0:T(8,128)(2,1)} %weight_grad.29), channel_id=1, source_target_pairs={{0,2},{2,0},{4,6},{6,4},{8,10},{10,8},{12,14},{14,12},{16,18},{18,... | collective-permute-start | bytes 3538952 | tf_op jit(solution)/shard_map/ppermute | solution.py:684
  237.9 70.6 %collective-permute-start.59 = (bf16[768,768]{1,0:T(8,128)(2,1)}, bf16[768,768]{1,0:T(8,128)(2,1)S(1)}, u32[]{:S(2)}, u32[]{:S(2)}) collective-permute-start(bf16[768,768]{1,0:T(8,128)(2,1)} %weight_grad.28), channel_id=1, source_target_pairs={{0,2},{2,0},{4,6},{6,4},{8,10},{10,8},{12,14},{14,12},{16,18},{18,... | collective-permute-start | bytes 3538952 | tf_op jit(solution)/shard_map/ppermute | solution.py:684
  242.8 44.3 %collective-permute-start.50 = (bf16[768,768]{1,0:T(8,128)(2,1)}, bf16[768,768]{1,0:T(8,128)(2,1)}, u32[]{:S(2)}, u32[]{:S(2)}) collective-permute-start(bf16[768,768]{1,0:T(8,128)(2,1)} %weight_grad.25), channel_id=1, source_target_pairs={{0,2},{2,0},{4,6},{6,4},{8,10},{10,8},{12,14},{14,12},{16,18},{18,... | collective-permute-start | bytes 3538952 | tf_op jit(solution)/shard_map/ppermute | solution.py:684
  247.6 86.4 %collective-permute-start.49 = (bf16[768,768]{1,0:T(8,128)(2,1)}, bf16[768,768]{1,0:T(8,128)(2,1)S(1)}, u32[]{:S(2)}, u32[]{:S(2)}) collective-permute-start(bf16[768,768]{1,0:T(8,128)(2,1)} %weight_grad.24), channel_id=1, source_target_pairs={{0,2},{2,0},{4,6},{6,4},{8,10},{10,8},{12,14},{14,12},{16,18},{18,... | collective-permute-start | bytes 3538952 | tf_op jit(solution)/shard_map/ppermute | solution.py:684
  280.4 41.2 %collective-permute-start.24 = (bf16[384,1152]{1,0:T(8,128)(2,1)}, bf16[384,1152]{1,0:T(8,128)(2,1)S(1)}, u32[]{:S(2)}, u32[]{:S(2)}) collective-permute-start(bf16[384,1152]{1,0:T(8,128)(2,1)} %weight_grad.17), channel_id=1, source_target_pairs={{0,2},{2,0},{4,6},{6,4},{8,10},{10,8},{12,14},{14,12},{16,18},{18,... | collective-permute-start | bytes 2654216 | tf_op jit(solution)/shard_map/ppermute | solution.py:684
  285.5 29.0 %collective-permute-start.61 = (bf16[768,768]{1,0:T(8,128)(2,1)}, bf16[768,768]{1,0:T(8,128)(2,1)S(1)}, u32[]{:S(2)}, u32[]{:S(2)}) collective-permute-start(bf16[768,768]{1,0:T(8,128)(2,1)} %weight_grad.30), channel_id=1, source_target_pairs={{0,1},{1,0},{2,3},{3,2},{4,5},{5,4},{6,7},{7,6},{8,9},{9,8},{10,11... | collective-permute-start | bytes 3538952 | tf_op jit(solution)/shard_map/ppermute | solution.py:681
  291.9 48.0 %collective-permute-start.51 = (bf16[768,768]{1,0:T(8,128)(2,1)}, bf16[768,768]{1,0:T(8,128)(2,1)}, u32[]{:S(2)}, u32[]{:S(2)}) collective-permute-start(bf16[768,768]{1,0:T(8,128)(2,1)} %weight_grad.26), channel_id=1, source_target_pairs={{0,1},{1,0},{2,3},{3,2},{4,5},{5,4},{6,7},{7,6},{8,9},{9,8},{10,11... | collective-permute-start | bytes 3538952 | tf_op jit(solution)/shard_map/ppermute | solution.py:681
  308.5 53.4 %collective-permute-start.23 = (bf16[384,1152]{1,0:T(8,128)(2,1)}, bf16[384,1152]{1,0:T(8,128)(2,1)}, u32[]{:S(2)}, u32[]{:S(2)}) collective-permute-start(bf16[384,1152]{1,0:T(8,128)(2,1)} %weight_grad.16), channel_id=1, source_target_pairs={{0,2},{2,0},{4,6},{6,4},{8,10},{10,8},{12,14},{14,12},{16,18},{18,... | collective-permute-start | bytes 2654216 | tf_op jit(solution)/shard_map/ppermute | solution.py:684
  321.3 24.4 %collective-permute-start.62 = (bf16[384,768]{1,0:T(8,128)(2,1)}, bf16[384,768]{1,0:T(8,128)(2,1)S(1)}, u32[]{:S(2)}, u32[]{:S(2)}) collective-permute-start(bf16[384,768]{1,0:T(8,128)(2,1)} %get-tuple-element.93), channel_id=1, source_target_pairs={{0,4},{2,6},{4,0},{6,2},{8,12},{10,14},{12,8},{14,10},{16,20},{18,... | collective-permute-start | bytes 1769480 | tf_op jit(solution)/shard_map/ppermute | solution.py:684
  327.4 34.9 %collective-permute-start.25 = (bf16[384,1152]{1,0:T(8,128)(2,1)}, bf16[384,1152]{1,0:T(8,128)(2,1)S(1)}, u32[]{:S(2)}, u32[]{:S(2)}) collective-permute-start(bf16[384,1152]{1,0:T(8,128)(2,1)} %weight_grad.18), channel_id=1, source_target_pairs={{0,1},{1,0},{2,3},{3,2},{4,5},{5,4},{6,7},{7,6},{8,9},{9,8},{10,11... | collective-permute-start | bytes 2654216 | tf_op jit(solution)/shard_map/ppermute | solution.py:681
  334.0 22.6 %collective-permute-start.40 = (bf16[384,384]{1,0:T(8,128)(2,1)}, bf16[384,384]{1,0:T(8,128)(2,1)}, u32[]{:S(2)}, u32[]{:S(2)}) collective-permute-start(bf16[384,384]{1,0:T(8,128)(2,1)} %weight_grad.21), channel_id=1, source_target_pairs={{0,2},{2,0},{4,6},{6,4},{8,10},{10,8},{12,14},{14,12},{16,18},{18,... | collective-permute-start | bytes 884744 | tf_op jit(solution)/shard_map/ppermute | solution.py:684
  339.9 7.7 %collective-permute-start.17 = (f32[1536]{0:T(1024)S(1)}, f32[1536]{0:T(1024)S(1)}, u32[]{:S(2)}, u32[]{:S(2)}) collective-permute-start(f32[1536]{0:T(1024)S(1)} %reshape.700), channel_id=1, source_target_pairs={{0,2},{2,0},{4,6},{6,4},{8,10},{10,8},{12,14},{14,12},{16,18},{18,... | collective-permute-start | bytes 18440 | tf_op jit(solution)/shard_map/ppermute | solution.py:684
  345.7 23.9 %collective-permute-start.52 = (bf16[384,768]{1,0:T(8,128)(2,1)}, bf16[384,768]{1,0:T(8,128)(2,1)S(1)}, u32[]{:S(2)}, u32[]{:S(2)}) collective-permute-start(bf16[384,768]{1,0:T(8,128)(2,1)} %get-tuple-element.89), channel_id=1, source_target_pairs={{0,4},{2,6},{4,0},{6,2},{8,12},{10,14},{12,8},{14,10},{16,20},{18,... | collective-permute-start | bytes 1769480 | tf_op jit(solution)/shard_map/ppermute | solution.py:684
  347.7 49.7 %collective-permute-start.63 = (bf16[384,768]{1,0:T(8,128)(2,1)S(1)}, bf16[384,768]{1,0:T(8,128)(2,1)S(1)}, u32[]{:S(2)}, u32[]{:S(2)}) collective-permute-start(bf16[384,768]{1,0:T(8,128)(2,1)S(1)} %add.199), channel_id=1, source_target_pairs={{0,8},{2,10},{4,12},{6,14},{24,16},{26,18},{28,20},{30,22},{1,9},{... | collective-permute-start | bytes 1769480 | tf_op jit(solution)/shard_map/ppermute | solution.py:696
  361.8 22.9 %collective-permute-start.39 = (bf16[384,384]{1,0:T(8,128)(2,1)S(1)}, bf16[384,384]{1,0:T(8,128)(2,1)S(1)}, u32[]{:S(2)}, u32[]{:S(2)}) collective-permute-start(bf16[384,384]{1,0:T(8,128)(2,1)S(1)} %copy-done.19), channel_id=1, source_target_pairs={{0,2},{2,0},{4,6},{6,4},{8,10},{10,8},{12,14},{14,12},{16,18},{18,... | collective-permute-start | bytes 884744 | tf_op jit(solution)/shard_map/ppermute | solution.py:684
  361.9 7.3 %collective-permute-start.33 = (f32[11736]{0:T(1024)S(1)}, f32[11736]{0:T(1024)S(1)}, u32[]{:S(2)}, u32[]{:S(2)}) collective-permute-start(f32[11736]{0:T(1024)S(1)} %concatenate.68), channel_id=1, source_target_pairs={{0,2},{2,0},{4,6},{6,4},{8,10},{10,8},{12,14},{14,12},{16,18},{18,... | collective-permute-start | bytes 140840 | tf_op jit(solution)/shard_map/ppermute | solution.py:684
  362.4 23.8 %collective-permute-start.41 = (bf16[384,384]{1,0:T(8,128)(2,1)}, bf16[384,384]{1,0:T(8,128)(2,1)S(1)}, u32[]{:S(2)}, u32[]{:S(2)}) collective-permute-start(bf16[384,384]{1,0:T(8,128)(2,1)} %weight_grad.22), channel_id=1, source_target_pairs={{0,1},{1,0},{2,3},{3,2},{4,5},{5,4},{6,7},{7,6},{8,9},{9,8},{10,11... | collective-permute-start | bytes 884744 | tf_op jit(solution)/shard_map/ppermute | solution.py:681
  369.2 34.8 %collective-permute-start.26 = (bf16[192,1152]{1,0:T(8,128)(2,1)}, bf16[192,1152]{1,0:T(8,128)(2,1)S(1)}, u32[]{:S(2)}, u32[]{:S(2)}) collective-permute-start(bf16[192,1152]{1,0:T(8,128)(2,1)} %get-tuple-element.76), channel_id=1, source_target_pairs={{0,4},{2,6},{4,0},{6,2},{8,12},{10,14},{12,8},{14,10},{16,20},{18,... | collective-permute-start | bytes 1327112 | tf_op jit(solution)/shard_map/ppermute | solution.py:684
  369.5 12.8 %collective-permute-start.34 = (f32[11736]{0:T(1024)S(1)}, f32[11736]{0:T(1024)S(1)}, u32[]{:S(2)}, u32[]{:S(2)}) collective-permute-start(f32[11736]{0:T(1024)S(1)} %add.187), channel_id=1, source_target_pairs={{0,4},{2,6},{4,0},{6,2},{8,12},{10,14},{12,8},{14,10},{16,20},{18,... | collective-permute-start | bytes 140840 | tf_op jit(solution)/shard_map/ppermute | solution.py:684
  382.3 38.6 %collective-permute-start.53 = (bf16[384,768]{1,0:T(8,128)(2,1)S(1)}, bf16[384,768]{1,0:T(8,128)(2,1)S(1)}, u32[]{:S(2)}, u32[]{:S(2)}) collective-permute-start(bf16[384,768]{1,0:T(8,128)(2,1)S(1)} %add.196), channel_id=1, source_target_pairs={{0,8},{2,10},{4,12},{6,14},{24,16},{26,18},{28,20},{30,22},{1,9},{... | collective-permute-start | bytes 1769480 | tf_op jit(solution)/shard_map/ppermute | solution.py:696
  384.7 12.3 %collective-permute-start.19 = (f32[1536]{0:T(1024)S(1)}, f32[1536]{0:T(1024)S(1)}, u32[]{:S(2)}, u32[]{:S(2)}) collective-permute-start(f32[1536]{0:T(1024)S(1)} %add.176), channel_id=1, source_target_pairs={{0,8},{2,10},{4,12},{6,14},{24,16},{26,18},{28,20},{30,22},{1,9},{... | collective-permute-start | bytes 18440 | tf_op jit(solution)/shard_map/ppermute | solution.py:696
  386.2 12.0 %collective-permute-start.35 = (f32[11736]{0:T(1024)S(1)}, f32[11736]{0:T(1024)S(1)}, u32[]{:S(2)}, u32[]{:S(2)}) collective-permute-start(f32[11736]{0:T(1024)S(1)} %add.188), channel_id=1, source_target_pairs={{0,8},{2,10},{4,12},{6,14},{24,16},{26,18},{28,20},{30,22},{1,9},{... | collective-permute-start | bytes 140840 | tf_op jit(solution)/shard_map/ppermute | solution.py:696
  397.0 5.4 %collective-permute-start.42 = (bf16[192,384]{1,0:T(8,128)(2,1)}, bf16[192,384]{1,0:T(8,128)(2,1)S(1)}, u32[]{:S(2)}, u32[]{:S(2)}) collective-permute-start(bf16[192,384]{1,0:T(8,128)(2,1)} %get-tuple-element.85), channel_id=1, source_target_pairs={{0,4},{2,6},{4,0},{6,2},{8,12},{10,14},{12,8},{14,10},{16,20},{18,... | collective-permute-start | bytes 442376 | tf_op jit(solution)/shard_map/ppermute | solution.py:684
  397.4 17.4 %collective-permute-start.20 = (f32[1536]{0:T(1024)S(1)}, f32[1536]{0:T(1024)S(1)}, u32[]{:S(2)}, u32[]{:S(2)}) collective-permute-start(f32[1536]{0:T(1024)S(1)} %add.177), channel_id=1, source_target_pairs={{8,16},{10,18},{12,20},{14,22},{16,8},{18,10},{20,12},{22,14},{9,1... | collective-permute-start | bytes 18440 | tf_op jit(solution)/shard_map/ppermute | solution.py:696
  398.2 28.7 %collective-permute-start.64 = (bf16[384,768]{1,0:T(8,128)(2,1)S(1)}, bf16[384,768]{1,0:T(8,128)(2,1)S(1)}, u32[]{:S(2)}, u32[]{:S(2)}) collective-permute-start(bf16[384,768]{1,0:T(8,128)(2,1)S(1)} %add.200), channel_id=1, source_target_pairs={{8,16},{10,18},{12,20},{14,22},{16,8},{18,10},{20,12},{22,14},{9,1... | collective-permute-start | bytes 1769480 | tf_op jit(solution)/shard_map/ppermute | solution.py:696
  402.3 14.2 %collective-permute-start.36 = (f32[11736]{0:T(1024)S(1)}, f32[11736]{0:T(1024)S(1)}, u32[]{:S(2)}, u32[]{:S(2)}) collective-permute-start(f32[11736]{0:T(1024)S(1)} %add.189), channel_id=1, source_target_pairs={{8,16},{10,18},{12,20},{14,22},{16,8},{18,10},{20,12},{22,14},{9,1... | collective-permute-start | bytes 140840 | tf_op jit(solution)/shard_map/ppermute | solution.py:696
  404.0 14.7 %collective-permute-start.43 = (bf16[192,384]{1,0:T(8,128)(2,1)S(1)}, bf16[192,384]{1,0:T(8,128)(2,1)}, u32[]{:S(2)}, u32[]{:S(2)}) collective-permute-start(bf16[192,384]{1,0:T(8,128)(2,1)S(1)} %add.193), channel_id=1, source_target_pairs={{0,8},{2,10},{4,12},{6,14},{24,16},{26,18},{28,20},{30,22},{1,9},{... | collective-permute-start | bytes 442376 | tf_op jit(solution)/shard_map/ppermute | solution.py:696
  414.7 10.5 %collective-permute-start.27 = (bf16[192,1152]{1,0:T(8,128)(2,1)S(1)}, bf16[192,1152]{1,0:T(8,128)(2,1)S(1)}, u32[]{:S(2)}, u32[]{:S(2)}) collective-permute-start(bf16[192,1152]{1,0:T(8,128)(2,1)S(1)} %add.180), channel_id=1, source_target_pairs={{0,8},{2,10},{4,12},{6,14},{24,16},{26,18},{28,20},{30,22},{1,9},{... | collective-permute-start | bytes 1327112 | tf_op jit(solution)/shard_map/ppermute | solution.py:696
  416.6 6.1 %collective-permute-start.21 = (f32[1536]{0:T(1024)S(1)}, f32[1536]{0:T(1024)S(1)}, u32[]{:S(2)}, u32[]{:S(2)}) collective-permute-start(f32[1536]{0:T(1024)S(1)} %add.178), channel_id=1, source_target_pairs={{8,0},{10,2},{12,4},{14,6},{16,24},{18,26},{20,28},{22,30},{9,1},{... | collective-permute-start | bytes 18440 | tf_op jit(solution)/shard_map/ppermute | solution.py:696
  418.6 9.1 %collective-permute-start.37 = (f32[11736]{0:T(1024)S(1)}, f32[11736]{0:T(1024)S(1)}, u32[]{:S(2)}, u32[]{:S(2)}) collective-permute-start(f32[11736]{0:T(1024)S(1)} %add.190), channel_id=1, source_target_pairs={{8,0},{10,2},{12,4},{14,6},{16,24},{18,26},{20,28},{22,30},{9,1},{... | collective-permute-start | bytes 140840 | tf_op jit(solution)/shard_map/ppermute | solution.py:696
  422.6 6.5 %collective-permute-start.54 = (bf16[384,768]{1,0:T(8,128)(2,1)S(1)}, bf16[384,768]{1,0:T(8,128)(2,1)S(1)}, u32[]{:S(2)}, u32[]{:S(2)}) collective-permute-start(bf16[384,768]{1,0:T(8,128)(2,1)S(1)} %add.197), channel_id=1, source_target_pairs={{8,16},{10,18},{12,20},{14,22},{16,8},{18,10},{20,12},{22,14},{9,1... | collective-permute-start | bytes 1769480 | tf_op jit(solution)/shard_map/ppermute | solution.py:696
  423.4 48.9 %collective-permute-start.22 = (f32[1536]{0:T(1024)S(1)}, f32[1536]{0:T(1024)S(1)}, u32[]{:S(2)}, u32[]{:S(2)}) collective-permute-start(f32[1536]{0:T(1024)S(1)} %broadcast_select_fusion.9), channel_id=1, source_target_pairs={{0,1},{1,0},{2,3},{3,2},{4,5},{5,4},{6,7},{7,6},{8,9},{9,8},{10,11... | collective-permute-start | bytes 18440 | tf_op jit(solution)/shard_map/ppermute | solution.py:681
  425.2 15.4 %collective-permute-start.45 = (bf16[192,384]{1,0:T(8,128)(2,1)S(1)}, bf16[192,384]{1,0:T(8,128)(2,1)S(1)}, u32[]{:S(2)}, u32[]{:S(2)}) collective-permute-start(bf16[192,384]{1,0:T(8,128)(2,1)S(1)} %add.195), channel_id=1, source_target_pairs={{8,0},{10,2},{12,4},{14,6},{16,24},{18,26},{20,28},{22,30},{9,1},{... | collective-permute-start | bytes 442376 | tf_op jit(solution)/shard_map/ppermute | solution.py:696
  426.9 14.0 %collective-permute-start.28 = (bf16[192,1152]{1,0:T(8,128)(2,1)S(1)}, bf16[192,1152]{1,0:T(8,128)(2,1)S(1)}, u32[]{:S(2)}, u32[]{:S(2)}) collective-permute-start(bf16[192,1152]{1,0:T(8,128)(2,1)S(1)} %add.181), channel_id=1, source_target_pairs={{8,16},{10,18},{12,20},{14,22},{16,8},{18,10},{20,12},{22,14},{9,1... | collective-permute-start | bytes 1327112 | tf_op jit(solution)/shard_map/ppermute | solution.py:696
  427.8 26.4 %collective-permute-start.65 = (bf16[384,768]{1,0:T(8,128)(2,1)S(1)}, bf16[384,768]{1,0:T(8,128)(2,1)S(1)}, u32[]{:S(2)}, u32[]{:S(2)}) collective-permute-start(bf16[384,768]{1,0:T(8,128)(2,1)S(1)} %add.201), channel_id=1, source_target_pairs={{8,0},{10,2},{12,4},{14,6},{16,24},{18,26},{20,28},{22,30},{9,1},{... | collective-permute-start | bytes 1769480 | tf_op jit(solution)/shard_map/ppermute | solution.py:696
  429.3 36.4 %collective-permute-start.55 = (bf16[384,768]{1,0:T(8,128)(2,1)S(1)}, bf16[384,768]{1,0:T(8,128)(2,1)S(1)}, u32[]{:S(2)}, u32[]{:S(2)}) collective-permute-start(bf16[384,768]{1,0:T(8,128)(2,1)S(1)} %add.198), channel_id=1, source_target_pairs={{8,0},{10,2},{12,4},{14,6},{16,24},{18,26},{20,28},{22,30},{9,1},{... | collective-permute-start | bytes 1769480 | tf_op jit(solution)/shard_map/ppermute | solution.py:696
  440.6 31.7 %collective-permute-start.38 = (f32[7404]{0:T(1024)S(1)}, f32[7404]{0:T(1024)}, u32[]{:S(2)}, u32[]{:S(2)}) collective-permute-start(f32[7404]{0:T(1024)S(1)} %pad_maximum_fusion.2), channel_id=1, source_target_pairs={{0,1},{1,0},{2,3},{3,2},{4,5},{5,4},{6,7},{7,6},{8,9},{9,8},{10,11... | collective-permute-start | bytes 88856 | tf_op jit(solution)/shard_map/ppermute | solution.py:681
  440.9 33.8 %collective-permute-start.46 = (bf16[192,384]{1,0:T(8,128)(2,1)S(1)}, bf16[192,384]{1,0:T(8,128)(2,1)}, u32[]{:S(2)}, u32[]{:S(2)}) collective-permute-start(bf16[192,384]{1,0:T(8,128)(2,1)S(1)} %broadcast_select_fusion.5.refs_0_), channel_id=1, source_target_pairs={{0,4},{2,6},{4,0},{6,2},{8,12},{10,14},{12,8},{14,10},{16,20},{18,... | collective-permute-start | bytes 442376 | tf_op jit(solution)/shard_map/ppermute | solution.py:684
  454.2 16.3 %collective-permute-start.29 = (bf16[192,1152]{1,0:T(8,128)(2,1)S(1)}, bf16[192,1152]{1,0:T(8,128)(2,1)S(1)}, u32[]{:S(2)}, u32[]{:S(2)}) collective-permute-start(bf16[192,1152]{1,0:T(8,128)(2,1)S(1)} %add.182), channel_id=1, source_target_pairs={{8,0},{10,2},{12,4},{14,6},{16,24},{18,26},{20,28},{22,30},{9,1},{... | collective-permute-start | bytes 1327112 | tf_op jit(solution)/shard_map/ppermute | solution.py:696
  465.7 30.2 %collective-permute-start.66 = (bf16[384,768]{1,0:T(8,128)(2,1)S(1)}, bf16[384,768]{1,0:T(8,128)(2,1)S(1)}, u32[]{:S(2)}, u32[]{:S(2)}) collective-permute-start(bf16[384,768]{1,0:T(8,128)(2,1)S(1)} %broadcast_select_fusion.refs_0_), channel_id=1, source_target_pairs={{0,4},{2,6},{4,0},{6,2},{8,12},{10,14},{12,8},{14,10},{16,20},{18,... | collective-permute-start | bytes 1769480 | tf_op jit(solution)/shard_map/ppermute | solution.py:684
  470.5 25.9 %collective-permute-start.56 = (bf16[384,768]{1,0:T(8,128)(2,1)S(1)}, bf16[384,768]{1,0:T(8,128)(2,1)S(1)}, u32[]{:S(2)}, u32[]{:S(2)}) collective-permute-start(bf16[384,768]{1,0:T(8,128)(2,1)S(1)} %broadcast_select_fusion.1.refs_0_), channel_id=1, source_target_pairs={{0,4},{2,6},{4,0},{6,2},{8,12},{10,14},{12,8},{14,10},{16,20},{18,... | collective-permute-start | bytes 1769480 | tf_op jit(solution)/shard_map/ppermute | solution.py:684
  472.3 23.6 %collective-permute-start.30 = (bf16[192,1152]{1,0:T(8,128)(2,1)S(1)}, bf16[192,1152]{1,0:T(8,128)(2,1)}, u32[]{:S(2)}, u32[]{:S(2)}) collective-permute-start(bf16[192,1152]{1,0:T(8,128)(2,1)S(1)} %broadcast_select_fusion.4.refs_0_), channel_id=1, source_target_pairs={{0,4},{2,6},{4,0},{6,2},{8,12},{10,14},{12,8},{14,10},{16,20},{18,... | collective-permute-start | bytes 1327112 | tf_op jit(solution)/shard_map/ppermute | solution.py:684
  474.9 23.9 %collective-permute-start.31 = (bf16[192,1152]{1,0:T(8,128)(2,1)S(1)}, bf16[192,1152]{1,0:T(8,128)(2,1)}, u32[]{:S(2)}, u32[]{:S(2)}) collective-permute-start(bf16[192,1152]{1,0:T(8,128)(2,1)S(1)} %broadcast_select_fusion.4.refs_0_), channel_id=1, source_target_pairs={{0,2},{2,0},{4,6},{6,4},{8,10},{10,8},{12,14},{14,12},{16,18},{18,... | collective-permute-start | bytes 1327112 | tf_op jit(solution)/shard_map/ppermute | solution.py:684
  476.3 33.8 %collective-permute-start.67 = (bf16[384,768]{1,0:T(8,128)(2,1)S(1)}, bf16[384,768]{1,0:T(8,128)(2,1)}, u32[]{:S(2)}, u32[]{:S(2)}) collective-permute-start(bf16[384,768]{1,0:T(8,128)(2,1)S(1)} %broadcast_select_fusion.refs_0_), channel_id=1, source_target_pairs={{0,2},{2,0},{4,6},{6,4},{8,10},{10,8},{12,14},{14,12},{16,18},{18,... | collective-permute-start | bytes 1769480 | tf_op jit(solution)/shard_map/ppermute | solution.py:684
  495.9 19.2 %collective-permute-start.57 = (bf16[384,768]{1,0:T(8,128)(2,1)S(1)}, bf16[384,768]{1,0:T(8,128)(2,1)S(1)}, u32[]{:S(2)}, u32[]{:S(2)}) collective-permute-start(bf16[384,768]{1,0:T(8,128)(2,1)S(1)} %broadcast_select_fusion.1.refs_0_), channel_id=1, source_target_pairs={{0,2},{2,0},{4,6},{6,4},{8,10},{10,8},{12,14},{14,12},{16,18},{18,... | collective-permute-start | bytes 1769480 | tf_op jit(solution)/shard_map/ppermute | solution.py:684
  495.9 14.3 %collective-permute-start.68 = (bf16[384,768]{1,0:T(8,128)(2,1)S(1)}, bf16[384,768]{1,0:T(8,128)(2,1)}, u32[]{:S(2)}, u32[]{:S(2)}) collective-permute-start(bf16[384,768]{1,0:T(8,128)(2,1)S(1)} %collective-permute-done.66.refs_1_), channel_id=1, source_target_pairs={{0,2},{2,0},{4,6},{6,4},{8,10},{10,8},{12,14},{14,12},{16,18},{18,... | collective-permute-start | bytes 1769480 | tf_op jit(solution)/shard_map/ppermute | solution.py:684
  496.4 18.7 %collective-permute-start.58 = (bf16[384,768]{1,0:T(8,128)(2,1)S(1)}, bf16[384,768]{1,0:T(8,128)(2,1)}, u32[]{:S(2)}, u32[]{:S(2)}) collective-permute-start(bf16[384,768]{1,0:T(8,128)(2,1)S(1)} %collective-permute-done.56.refs_1_), channel_id=1, source_target_pairs={{0,2},{2,0},{4,6},{6,4},{8,10},{10,8},{12,14},{14,12},{16,18},{18,... | collective-permute-start | bytes 1769480 | tf_op jit(solution)/shard_map/ppermute | solution.py:684
  (46 other events, 556.7 us)
